TPU v7x, 256 devices: a whole 4x4x8 slice. The times are simulated.
256 devices in a mesh: grp: 8 (over y, core), span: 32 (over z, x).
Axes of the slice: x: 4, y: 4, z: 8, core: 2. Of those that a mesh axis runs over, the one named last changes fastest.
Arguments:
- record: float32 [1048576, 128], P(('grp', 'span')), may hold values from -96 to 96, as said below
Outputs:
- triangle: float32 [512, 512], replicated
- operator: float32 [512, 512], replicated
Inputs may be any that keep to these rules, and one draw needn't show every extreme that they name: `record`: Real-valued probe samples.
All inputs are finite; a program needn't handle non-finite values.
Results may differ from a plain program's by a relative error of at most 0.0003.
Values sent between devices are 32-bit elements; how exact they have to be, the bound alone decides.
No kernel may reach another device: no remote copies, remote signals or barrier semaphores. Data moves between devices by JAX's collectives and lax.ppermute only.
A program may use at most 64 MiB of HBM per device.

v0:
```python
import jax
import jax.numpy as jnp
from jax import lax
from jax.sharding import PartitionSpec as P

LAGS = 4
DELAY = 1024


def shifted(value, axis, steps):
    count = lax.axis_size(axis)
    leading, last = (max(0, -steps), min(count, count - steps))
    return lax.ppermute(value, axis, [(source, source + steps) for source in range(leading, last)])


def inner_rows(left, right):
    return lax.dot_general(
        left,
        right,
        (((0,), (0,)), ((), ())),
        precision=lax.Precision.HIGHEST,
        preferred_element_type=jnp.float32,
    )


def on_device(record):
    count = record.shape[0]
    lead = (LAGS - 1) * DELAY + 1
    following = shifted(record[:lead], ("grp", "span"), -1)
    ext = jnp.concatenate([record, following], 0)
    hank = jnp.concatenate([ext[k * DELAY : k * DELAY + count + 1] for k in range(LAGS)], 1)
    devices = lax.axis_size(("grp", "span"))
    last_row = count * devices - lead
    times = lax.axis_index(("grp", "span")) * count + jnp.arange(count, dtype=jnp.int32)
    weight = (
        jnp.where(times < last_row, 1.0, 0.0)
        - 0.5 * jnp.where(times == 0, 1.0, 0.0)
        - 0.5 * jnp.where(times == last_row, 1.0, 0.0)
    )
    weight = weight.astype(jnp.float32)
    inside = jnp.where(times < last_row, 1.0, 0.0).astype(jnp.float32)
    head = hank[:count]
    weighted = head * weight[:, None]
    cross = inner_rows(head * inside[:, None], hank[1 : count + 1])
    scale = 1.0 / last_row
    gram = inner_rows(weighted, head)
    gram, cross = lax.psum((gram, cross), ("grp", "span"))
    lower = jnp.linalg.cholesky(gram * scale)
    middle = jax.scipy.linalg.solve_triangular(lower, cross * scale, lower=True)
    operator = jax.scipy.linalg.solve_triangular(lower, middle.T, lower=True).T
    return (lower.T, operator)


def solution(mesh):
    placed = (P(("grp", "span"), None),)
    return jax.shard_map(
        on_device, mesh=mesh, in_specs=placed, out_specs=(P(), P()), check_vma=False
    )
```

profile of v0, /device:TPU:1, one launch (start us, length us, event | category | flops | bytes accessed | tf_op | source)
XLA Modules:
  0.0 505.2 jit_solution(4114542410660674307)
XLA Ops:
  7.2 1.5 slice.124
  8.7 11.1 %collective-permute-start = (f32[3073,128]{1,0:T(8,128)S(1)}, f32[3073,128]{1,0:T(8,128)S(1)}, u32[]{:S(2)}, u32[]{:S(2)}) collective-permute-start(f32[3073,128]{1,0:T(8,128)S(1)} %slice.124), channel_id=1, source_target_pairs={{1,0},{2,1},{3,2},{4,3},{5,4},{6,5},{7,6},{8,7},{9,8},{10,9},{11,1... | collective-permute-start | bytes 4720136 | tf_op jit(solution)/shard_map/ppermute | solution.py:13
  19.8 1.7 constant_dynamic-update-slice_fusion.1
  21.6 23.0 %collective-permute-done = f32[3073,128]{1,0:T(8,128)S(1)} collective-permute-done((f32[3073,128]{1,0:T(8,128)S(1)}, f32[3073,128]{1,0:T(8,128)S(1)}, u32[]{:S(2)}, u32[]{:S(2)}) %collective-permute-start) | collective-permute-done | bytes 1573408 | tf_op jit(solution)/shard_map/ppermute | solution.py:13
  44.6 0.5 fusion.64
  45.2 1.4 pad_maximum_fusion
  46.6 17.3 %fusion.2 = f32[512,512]{0,1:T(8,128)} fusion(f32[4097,512]{1,0:T(8,128)S(1)} %pad_maximum_fusion, f32[4096]{0:T(1024)S(1)} %get-tuple-element.52), kind=kOutput, calls=%fused_computation.5 | convolution fusion | flops 12886999040 | bytes 17842176 | tf_op jit(solution)/shard_map/dot_general | solution.py:17
  63.8 16.4 %fusion = f32[512,512]{0,1:T(8,128)} fusion(f32[4097,512]{1,0:T(8,128)S(1)} %pad_maximum_fusion, f32[4096]{0:T(1024)S(1)} %get-tuple-element.51), kind=kOutput, calls=%fused_computation.2 | convolution fusion | flops 12886999040 | bytes 17842176 | tf_op jit(solution)/shard_map/dot_general | solution.py:17
  80.2 269.1 %all-reduce.4.cloned.1.call-done = (f32[512,512]{0,1:T(8,128)}, f32[512,512]{0,1:T(8,128)}) async-done(((f32[512,512]{0,1:T(8,128)}, f32[512,512]{0,1:T(8,128)}), (f32[512,512]{0,1:T(8,128)}, f32[512,512]{0,1:T(8,128)})) %all-reduce.4.cloned.1.call-update) | async-done | bytes 2097168 | tf_op jit(solution)/shard_map/psum | solution.py:47
  349.3 1.3 broadcast_multiply_fusion.1
  351.0 1.5 fusion.9
  352.5 11.7 %cholesky.104 = f32[128,128]{1,0:T(8,128)S(1)} custom-call(f32[128,128]{1,0:T(8,128)S(1)} %cholesky.266), custom_call_target="Cholesky" | custom-call | tf_op jit(solution)/shard_map/jit(cholesky)/cholesky | solution.py:48
  364.2 9.8 %custom-call.30 = f32[1,128,128]{1,2,0:T(8,128)S(1)} custom-call(f32[1,128,128]{2,1,0:T(8,128)S(1)} %get-tuple-element.48), custom_call_target="InvertDiagBlocksLowerTriangular" | custom-call | tf_op jit(solution)/shard_map/jit(cholesky)/cholesky | solution.py:48
  374.8 12.2 %cholesky.217 = f32[128,128]{1,0:T(8,128)S(1)} custom-call(f32[128,128]{1,0:T(8,128)S(1)} %cholesky.270), custom_call_target="Cholesky" | custom-call | tf_op jit(solution)/shard_map/jit(cholesky)/cholesky | solution.py:48
  387.0 0.6 compare_reduce_fusion.2
  387.7 0.6 compare_reduce_fusion.3
  388.3 9.8 %custom-call.31 = f32[1,128,128]{1,2,0:T(8,128)S(1)} custom-call(f32[1,128,128]{2,1,0:T(8,128)S(1)} %get-tuple-element.45), custom_call_target="InvertDiagBlocksLowerTriangular" | custom-call | tf_op jit(solution)/shard_map/jit(cholesky)/cholesky | solution.py:48
  398.8 11.7 %cholesky.238 = f32[128,128]{1,0:T(8,128)S(1)} custom-call(f32[128,128]{1,0:T(8,128)S(1)} %cholesky.275), custom_call_target="Cholesky" | custom-call | tf_op jit(solution)/shard_map/jit(cholesky)/cholesky | solution.py:48
  410.5 0.7 compare_reduce_fusion.1
  411.3 9.8 %custom-call.32 = f32[1,128,128]{1,2,0:T(8,128)S(1)} custom-call(f32[1,128,128]{2,1,0:T(8,128)S(1)} %get-tuple-element.42), custom_call_target="InvertDiagBlocksLowerTriangular" | custom-call | tf_op jit(solution)/shard_map/jit(cholesky)/cholesky | solution.py:48
  421.7 11.9 %cholesky.255 = f32[128,128]{1,0:T(8,128)S(1)} custom-call(f32[128,128]{1,0:T(8,128)S(1)} %convolution_subtract_fusion.8), custom_call_target="Cholesky" | custom-call | tf_op jit(solution)/shard_map/jit(cholesky)/cholesky | solution.py:48
  433.6 0.6 compare_reduce_fusion
  437.1 8.0 %while.4 = (s32[]{:T(128)}, f32[512,512]{1,0:T(8,128)S(1)}, s32[4,2]{0,1:T(2,128)S(1)}, f32[4,128,128]{2,1,0:T(8,128)S(1)}, s32[]{:T(128)}) while((s32[]{:T(128)}, f32[512,512]{1,0:T(8,128)S(1)}, s32[4,2]{0,1:T(2,128)S(1)}, f32[4,128,128]{2,1,0:T(8,128)S(1)}, s32[]{:T(128)}) %tuple.41), condition=%wide.while_cond.clone, body=%wide.while_body.clone.sunk | while | flops 2 | bytes 131181 | solution.py:50
  437.1 0.5 fusion.75
  437.7 1.4 bitcast_dynamic-update-slice_fusion.2
  439.1 0.5 fusion.75
  439.7 1.4 bitcast_dynamic-update-slice_fusion.2
  441.1 0.5 fusion.75
  441.7 1.4 bitcast_dynamic-update-slice_fusion.2
  443.1 0.5 fusion.75
  443.7 1.4 bitcast_dynamic-update-slice_fusion.2
  445.1 39.3 %custom-call.35 = f32[4,128,128]{1,2,0:T(8,128)S(1)} custom-call(f32[4,128,128]{2,1,0:T(8,128)S(1)} %get-tuple-element.18), custom_call_target="InvertDiagBlocksLowerTriangular" | custom-call | tf_op jit(solution)/shard_map/jit(_solve_triangular)/triangular_solve | solution.py:50
  484.4 1.3 broadcast_multiply_fusion
  485.7 0.4 fusion.30
  486.2 0.6 convolution_subtract_fusion.3
  486.8 0.4 fusion.48
  487.2 1.0 convolution_subtract_fusion.2
  488.2 0.4 fusion.50
  488.6 1.5 convolution_subtract_fusion.5
  490.1 0.4 fusion.52
  490.6 0.4 fusion.28
  491.1 0.6 convolution_subtract_fusion.1
  491.7 0.4 fusion.47
  492.1 1.0 convolution_subtract_fusion
  493.5 1.5 convolution_subtract_fusion.4
  495.0 0.4 fusion.51
  495.5 1.3 copy.7
  496.9 1.3 copy.6
  (30 shorter events, 3.8 us)
Async XLA Ops:
  7.2 342.1 %all-reduce.4.cloned.1.call-start = ((), (), s32[]{:S(2)}) async-start(), calls=%async_computation | async-start | bytes 4194304 | tf_op jit(solution)/shard_map/psum | solution.py:47
  8.7 35.8 %collective-permute-start = (f32[3073,128]{1,0:T(8,128)S(1)}, f32[3073,128]{1,0:T(8,128)S(1)}, u32[]{:S(2)}, u32[]{:S(2)}) collective-permute-start(f32[3073,128]{1,0:T(8,128)S(1)} %slice.124), channel_id=1, source_target_pairs={{1,0},{2,1},{3,2},{4,3},{5,4},{6,5},{7,6},{8,7},{9,8},{10,9},{11,1... | collective-permute-start | bytes 4720136 | tf_op jit(solution)/shard_map/ppermute | solution.py:13
Sparse Core Ops, SparseCore 0:
  80.3 268.9 all-reduce.3
where the time goes:
time: 511 us; the launch traced here: 505 us
  waiting for transfers between devices  292 us (57%)
  other arithmetic  125 us (24%)
  matrix products  45 us (9%)
  between operations  17.1 us (3%)
  local copies, waits for them, and re-layouts  14.9 us (3%)
  starting transfers between devices  11.1 us (2%)
    psum x1, waiting for transfers between devices, on_device(): gram, cross = lax.psum((gram, cross), ('grp', 'span'))  269 us
    another operation x15, other arithmetic, on_device(): lower = jnp.linalg.cholesky(gram * scale)  79.7 us
    another operation x4, other arithmetic, on_device(): operator = jax.scipy.linalg.solve_triangular(lower, middle.T, lower=True).T  39.6 us
    dot_general x2, matrix products, inner_rows(): lax.dot_general(left, right, (((0,), (0,)), ((), ())), precision=lax.Prec...  33.6 us
    ppermute x1, waiting for transfers between devices, shifted(): lax.ppermute(value, axis, [(source, source + steps) for source in range(l...  23 us
    ppermute x1, starting transfers between devices, shifted(): lax.ppermute(value, axis, [(source, source + steps) for source in range(l...  11.1 us
  transfers between devices with their start and end apart: 2, of which 2 were waited for; matrix products, arithmetic and copies ran while one was open for 0% of the time, Pallas kernels for 0%

commit v1 on v0

v1 whole, which is shorter than its diff:
```python
import functools

import jax
import jax.numpy as jnp
from jax import lax
from jax.experimental import pallas as pl
from jax.experimental.pallas import tpu as pltpu
from jax.sharding import PartitionSpec as P

LAGS = 4
DELAY = 1024
N = 128
COLS = LAGS * N
HALF = DELAY // 2
SPAN = DELAY + HALF
AXES = ("grp", "span")
HIGHEST = lax.Precision.HIGHEST
VMEM_LIMIT = 48 * 2**20

PAIRS = [(i, j) for i in range(LAGS) for j in range(i, LAGS)]
GRAM = {pair: index for index, pair in enumerate(PAIRS)}
CROSS = {(i, j): len(PAIRS) + LAGS * i + j for i in range(LAGS) for j in range(LAGS)}
BLOCKS = len(GRAM) + len(CROSS)


def exact(left, right, dims):
    return lax.dot_general(left, right, (dims, ((), ())), precision=HIGHEST, preferred_element_type=jnp.float32)


def rows_product(left, right):
    return lax.dot_general(left, right, (((0,), (0,)), ((), ())), preferred_element_type=jnp.float32)


def parts(value):
    high = value.astype(jnp.bfloat16)
    low = (value - high.astype(jnp.float32)).astype(jnp.bfloat16)
    return jnp.concatenate([high, low], 1)


def fold(value):
    return (value[:N, :N] + value[N:, :N]) + (value[:N, N:] + value[N:, N:])


def lag_products(left, right, zero_lag=False):
    first = rows_product(left, right[:, : 2 * N])
    same, back = fold(first[: 2 * N]), fold(first[2 * N :])
    ahead = None if zero_lag else fold(rows_product(left[:, : 2 * N], right[:, 2 * N :]))
    return same, back, ahead


def local_kernel(edge_ref, rec_ref, out_ref, split_ref, same_ref, back_ref, ahead_ref):
    count = rec_ref.shape[0]
    for q in range(LAGS):
        lo, hi = q * DELAY, (q + 1) * DELAY
        split_ref[lo:hi, : 2 * N] = parts(rec_ref[lo:hi, :])
        if q < LAGS - 1:
            following = rec_ref[lo + 1 : hi + 1, :]
        else:
            following = jnp.concatenate([rec_ref[lo + 1 : hi, :], jnp.zeros((1, N), jnp.float32)], 0)
        split_ref[lo:hi, 2 * N :] = parts(following)
    for q in range(LAGS):
        left = split_ref[q * DELAY : (q + 1) * DELAY, :]
        for d in range(LAGS - q):
            right = split_ref[(q + d) * DELAY : (q + d + 1) * DELAY, :]
            same, back, ahead = lag_products(left, right, d == 0)
            same_ref[LAGS * q + d] = same
            back_ref[LAGS * q + d] = back
            if d:
                ahead_ref[LAGS * q + d] = ahead
    first, last = edge_ref[0], edge_ref[1]

    def kept(q, m):
        if q < m:
            return (1 - first).astype(jnp.float32)
        if q > m:
            return (1 - last).astype(jnp.float32)
        return None

    def total(ref, d, m):
        value = None
        for q in range(LAGS - d):
            factor, term = kept(q, m), ref[LAGS * q + d]
            term = term if factor is None else term * factor
            value = term if value is None else value + term
        return value

    for i, j in PAIRS:
        d = j - i
        out_ref[GRAM[i, j]] = total(same_ref, d, i)
        out_ref[CROSS[j, i]] = total(back_ref, d, i)
        if d:
            out_ref[CROSS[i, j]] = total(ahead_ref, d, i)

    @pl.when(first + last > 0)
    def _():
        def wide(offset, steps):
            pieces = [rec_ref[offset + k * DELAY : offset + k * DELAY + 1, :] for k in range(steps)]
            pieces += [jnp.zeros((1, N), jnp.float32)] * (LAGS - steps)
            return jnp.concatenate(pieces, 1)

        start = wide(0, LAGS) * first.astype(jnp.float32)
        final = wide(DELAY - 1, LAGS) * last.astype(jnp.float32)
        after = wide(DELAY, LAGS - 1)
        blank = jnp.zeros((6, COLS), jnp.float32)
        ends = jnp.concatenate([start, final, blank], 0)
        steps = jnp.concatenate([jnp.zeros((1, COLS), jnp.float32), after, blank], 0)
        outer = ((0,), (0,))
        for i in range(LAGS):
            for j in range(LAGS):
                a, b = ends[:, i * N : (i + 1) * N], ends[:, j * N : (j + 1) * N]
                c = steps[:, j * N : (j + 1) * N]
                if j >= i:
                    out_ref[GRAM[i, j]] -= 0.5 * exact(a, b, outer)
                out_ref[CROSS[i, j]] -= exact(c, a, outer) if i >= j else exact(a, c, outer)


def halo_kernel(edge_ref, acc_ref, split_ref, down_ref, up_ref, out_ref, below, above):
    below[:, : 2 * N] = parts(down_ref[:SPAN, :])
    below[:, 2 * N :] = parts(down_ref[1 : SPAN + 1, :])
    above[:, : 2 * N] = parts(up_ref[...])
    own = split_ref[0:16, : 2 * N].astype(jnp.float32)[0:1]
    own = (own[:, :N] + own[:, N:]) * (1 - edge_ref[0]).astype(jnp.float32)
    above[:, 2 * N :] = parts(jnp.concatenate([up_ref[1:SPAN, :], own], 0))

    def own_rows(start, size):
        return split_ref[start : start + size, :]

    pairs = {
        1: [(own_rows(3 * DELAY, DELAY), below[:DELAY, :])],
        2: [(own_rows(2 * DELAY, DELAY), below[:DELAY, :]), (above[HALF:, :], own_rows(DELAY, DELAY))],
        3: [
            (own_rows(DELAY, DELAY), below[:DELAY, :]),
            (above[HALF:, :], own_rows(2 * DELAY, DELAY)),
            (own_rows(2 * DELAY, HALF), below[DELAY:, :]),
            (above[:HALF, :], own_rows(DELAY + HALF, HALF)),
        ],
    }
    lastrow = lax.broadcasted_iota(jnp.int32, (16, N), 0) == 15
    entering = parts(jnp.where(lastrow, jnp.broadcast_to(down_ref[0:1, :], (16, N)), 0.0))
    count = LAGS * DELAY
    fix = fold(rows_product(entering, split_ref[count - 16 : count, : 2 * N]))
    for i in range(LAGS):
        out_ref[GRAM[i, i]] = acc_ref[GRAM[i, i]]
        out_ref[CROSS[i, i]] = acc_ref[CROSS[i, i]] + fix
    for d in range(1, LAGS):
        stop = (LAGS - d) * DELAY
        same = None
        back = fold(rows_product(entering, below[DELAY - 16 : DELAY, : 2 * N])) if d == 1 else None
        ahead = fold(rows_product(split_ref[stop - 16 : stop, : 2 * N], entering))
        for left, right in pairs[d]:
            s, b, a = lag_products(left, right)
            same = s if same is None else same + s
            back = b if back is None else back + b
            ahead = ahead + a
        for i in range(LAGS - d):
            j = i + d
            out_ref[GRAM[i, j]] = acc_ref[GRAM[i, j]] + same
            out_ref[CROSS[j, i]] = acc_ref[CROSS[j, i]] + back
            out_ref[CROSS[i, j]] = acc_ref[CROSS[i, j]] + ahead


def lanes(value, j):
    return jnp.broadcast_to(value[:, j : j + 1], (value.shape[0], N))


def line(value, t, n):
    return jnp.broadcast_to(value[t : t + 1, :], (n, N))


def factor(rest, inverse):
    sub = lax.broadcasted_iota(jnp.int32, (8, N), 0)
    lane = lax.broadcasted_iota(jnp.int32, (8, N), 1)
    uppers, inverses = [], []
    for k in range(N // 8):
        n = rest.shape[0] - 8
        top, top_inverse = rest[:8], inverse[:8]
        cols = [lanes(top, 8 * k + t) for t in range(8)]
        if n:
            rest, inverse = rest[8:], inverse[8:]
            below = [lanes(rest, 8 * k + t) for t in range(8)]
        pivots = jnp.zeros((8, N), jnp.float32)
        for t in range(8):
            pivot = line(cols[t], t, 8)
            recip = 1.0 / pivot
            mult = jnp.where(sub > t, cols[t] * recip, 0.0)
            if n:
                mult_below = below[t] * jnp.broadcast_to(recip[:1], (n, N))
            for u in range(t + 1, 8):
                entry = cols[u][t : t + 1, :]
                if n:
                    below[u] = below[u] - mult_below * jnp.broadcast_to(entry, (n, N))
                cols[u] = cols[u] - mult * jnp.broadcast_to(entry, (8, N))
            pivots = jnp.where(sub == t, pivot, pivots)
            if n:
                rest = rest - mult_below * line(top, t, n)
                inverse = inverse - mult_below * line(top_inverse, t, n)
            top = top - mult * line(top, t, 8)
            top_inverse = top_inverse - mult * line(top_inverse, t, 8)
        root = lax.rsqrt(pivots)
        uppers.append(jnp.where(lane >= sub + 8 * k, top * root, 0.0))
        inverses.append(top_inverse * root)
    return jnp.concatenate(uppers, 0), jnp.concatenate(inverses, 0)


def tail_kernel(scale, sum_ref, tri_ref, op_ref, work, right, inv):
    for i in range(LAGS):
        for j in range(LAGS):
            if j >= i:
                work[i, :, j * N : (j + 1) * N] = sum_ref[GRAM[i, j]] * scale
            block = sum_ref[CROSS[i, j]]
            work[i, :, COLS + j * N : COLS + (j + 1) * N] = (block.T if i >= j else block) * scale
    rows = lax.broadcasted_iota(jnp.int32, (N, N), 0)
    eye = jnp.where(rows == lax.broadcasted_iota(jnp.int32, (N, N), 1), 1.0, 0.0).astype(jnp.float32)
    for k in range(LAGS):
        for j in range(k):
            tri_ref[k * N : (k + 1) * N, j * N : (j + 1) * N] = jnp.zeros((N, N), jnp.float32)

    def finish(k, upper, inverse):
        tri_ref[k * N : (k + 1) * N, k * N : (k + 1) * N] = upper
        solved = exact(inverse, work[k, :, (k + 1) * N :], ((1,), (0,)))
        work[k, :, (k + 1) * N :] = solved
        if k < LAGS - 1:
            tri_ref[k * N : (k + 1) * N, (k + 1) * N :] = solved[:, : (LAGS - 1 - k) * N]
        for i in range(k + 1, LAGS):
            lo = (i - k - 1) * N
            work[i, :, i * N :] = work[i, :, i * N :] - exact(solved[:, lo : lo + N], solved[:, lo:], ((0,), (0,)))

    def step(k, carry):
        upper, inverse = factor(work[k, :, pl.ds(pl.multiple_of(k * N, N), N)], eye)
        inv[k] = inverse
        for which in range(LAGS):
            pl.when(k == which)(functools.partial(finish, which, upper, inverse))
        return carry

    lax.fori_loop(0, LAGS, step, 0)
    for i in range(LAGS):
        right[i * N : (i + 1) * N, :] = work[i, :, COLS:]
    for j in range(LAGS):
        lo, hi = j * N, (j + 1) * N
        solved = exact(right[:, lo:hi], inv[j], ((1,), (1,)))
        op_ref[:, lo:hi] = solved
        if j < LAGS - 1:
            right[:, hi:] = right[:, hi:] - exact(solved, tri_ref[lo:hi, hi:], ((1,), (0,)))


def shifted(value, steps):
    count = lax.axis_size(AXES)
    leading, last = (max(0, -steps), min(count, count - steps))
    return lax.ppermute(value, AXES, [(source, source + steps) for source in range(leading, last)])


def spread_sum(value):
    pieces = lax.psum(tuple(value[r : r + 32] for r in range(0, value.shape[0], 32)), AXES)
    return jnp.concatenate(pieces, 0)


def averaged_blocks(record):
    count = record.shape[0]
    devices = lax.axis_size(AXES)
    index = lax.axis_index(AXES)
    edge = jnp.stack([index == 0, index == devices - 1]).astype(jnp.int32)
    down = shifted(record[: SPAN + 8], -1)
    up = shifted(record[count - SPAN :], 1)
    smem, vmem = pl.BlockSpec(memory_space=pltpu.SMEM), pl.BlockSpec(memory_space=pltpu.VMEM)
    params = pltpu.CompilerParams(vmem_limit_bytes=VMEM_LIMIT)
    block = jax.ShapeDtypeStruct((BLOCKS, N, N), jnp.float32)
    local, split = pl.pallas_call(
        local_kernel,
        out_shape=[block, jax.ShapeDtypeStruct((count, 4 * N), jnp.bfloat16)],
        in_specs=[smem, vmem],
        out_specs=[vmem, vmem],
        scratch_shapes=[pltpu.VMEM((LAGS * LAGS, N, N), jnp.float32)] * 3,
        compiler_params=params,
        cost_estimate=pl.CostEstimate(flops=4 * 10**9, bytes_accessed=8 * 2**20, transcendentals=0),
        name="local_products",
    )(edge, record)
    summed = pl.pallas_call(
        halo_kernel,
        out_shape=block,
        in_specs=[smem, vmem, vmem, vmem, vmem],
        out_specs=vmem,
        scratch_shapes=[pltpu.VMEM((SPAN, 4 * N), jnp.bfloat16)] * 2,
        compiler_params=params,
        cost_estimate=pl.CostEstimate(flops=3 * 10**9, bytes_accessed=9 * 2**20, transcendentals=0),
        name="halo_products",
    )(edge, local, split, down, up)
    return spread_sum(summed.reshape(BLOCKS * N, N)).reshape(BLOCKS, N, N)


def on_device(record):
    last_row = record.shape[0] * lax.axis_size(AXES) - (LAGS - 1) * DELAY - 1
    total = averaged_blocks(record)
    vmem = pl.BlockSpec(memory_space=pltpu.VMEM)
    square = jax.ShapeDtypeStruct((COLS, COLS), jnp.float32)
    return tuple(
        pl.pallas_call(
            functools.partial(tail_kernel, 1.0 / last_row),
            out_shape=[square, square],
            in_specs=[vmem],
            out_specs=[vmem, vmem],
            scratch_shapes=[
                pltpu.VMEM((LAGS, N, 2 * COLS), jnp.float32),
                pltpu.VMEM((COLS, COLS), jnp.float32),
                pltpu.VMEM((LAGS, N, N), jnp.float32),
            ],
            compiler_params=pltpu.CompilerParams(vmem_limit_bytes=VMEM_LIMIT),
            name="factor_and_solve",
        )(total)
    )


def solution(mesh):
    placed = (P(AXES, None),)
    return jax.shard_map(on_device, mesh=mesh, in_specs=placed, out_specs=(P(), P()), check_vma=False)
```

time: 511 us -> 161 us (0.32); the launches traced: 505 us -> 161 us
  waiting for transfers between devices: 292 us -> 17 us
  other arithmetic: 125 us -> 0.08 us
  blocking collectives: 0 us -> 87.7 us
  matrix products: 45 us -> 0 us
  Pallas kernels: 0 us -> 36.8 us
  between operations: 17.1 us -> 1.55 us
  local copies, waits for them, and re-layouts: 14.9 us -> 4.82 us
    psum x1 -> x0, waiting for transfers between devices: 269 us -> none  [on_device(): gram, cross = lax.psum((gram, cross), ('grp', 'span'))]
    another operation x19 -> x0, other arithmetic: 119 us -> none  [the longest x15 79.7 us: on_device(): lower = jnp.linalg.cholesky(gram * scale)]
    psum x0 -> x1, blocking collectives: none -> 87.7 us  [spread_sum(): lax.psum(tuple((value[r:r + 32] for r in range(0, value.shape[0], 32))),...]
    pallas_call x0 -> x3, Pallas kernels: none -> 36.8 us  [the longest x1 25.3 us: on_device(): pl.pallas_call(functools.partial(tail_kernel, 1.0 / last_row), out_shape=...]
    dot_general x2 -> x0, matrix products: 33.6 us -> none  [inner_rows(): lax.dot_general(left, right, (((0,), (0,)), ((), ())), precision=lax.Prec...]
    another operation x20 -> x0, matrix products: 11.4 us -> none  [the longest x7 4.78 us: on_device(): operator = jax.scipy.linalg.solve_triangular(lower, middle.T, lower=True).T]
    another operation x17 -> x0, local copies, waits for them, and re-layouts: 8.06 us -> none  [the longest x13 7.92 us: on_device(): operator = jax.scipy.linalg.solve_triangular(lower, middle.T, lower=True).T]
    ppermute x1 -> x2, waiting for transfers between devices: 23 us -> 17 us  [shifted(): lax.ppermute(value, AXES, [(source, source + steps) for source in range(l...]
  transfers between devices with their start and end apart: 2 -> 2, of which waited for: 2 -> 1; matrix products, arithmetic and copies ran while one was open for 0% -> 1% of each run, Pallas kernels for 0% -> 4%
where the time goes in v1:
time: 161 us
  blocking collectives  87.7 us (54%)
  Pallas kernels  36.8 us (23%)
  waiting for transfers between devices  17 us (11%)
  starting transfers between devices  13 us (8%)
  local copies, waits for them, and re-layouts  4.82 us (3%)
    psum x1, blocking collectives, spread_sum(): lax.psum(tuple((value[r:r + 32] for r in range(0, value.shape[0], 32))),...  87.7 us
    pallas_call x1, Pallas kernels, on_device(): pl.pallas_call(functools.partial(tail_kernel, 1.0 / last_row), out_shape=...  25.3 us
    ppermute x2, waiting for transfers between devices, shifted(): lax.ppermute(value, AXES, [(source, source + steps) for source in range(l...  17 us
    ppermute x2, starting transfers between devices, shifted(): lax.ppermute(value, AXES, [(source, source + steps) for source in range(l...  13 us
    pallas_call x1, Pallas kernels, averaged_blocks(): pl.pallas_call(local_kernel, out_shape=[block, jax.ShapeDtypeStruct((coun...  6.26 us
    pallas_call x1, Pallas kernels, averaged_blocks(): pl.pallas_call(halo_kernel, out_shape=block, in_specs=[smem, vmem, vmem,...  5.22 us
  transfers between devices with their start and end apart: 2, of which 1 were waited for; matrix products, arithmetic and copies ran while one was open for 1% of the time, Pallas kernels for 4%

profile of v1, /device:TPU:1, one launch (start us, length us, event | category | flops | bytes accessed | tf_op | source)
XLA Modules:
  0.0 161.0 jit_solution(12024150422664344334)
XLA Ops:
  0.6 0.0 copy-start
  0.6 2.2 %slice.318 = f32[1544,128]{1,0:T(8,128)} slice(f32[4096,128]{1,0:T(8,128)} %rec_ref.1), slice={[0:1544], [0:128]} | slice | bytes 1581056 | tf_op jit(solution)/shard_map/slice | solution.py:262
  2.9 11.1 %collective-permute-start = (f32[1544,128]{1,0:T(8,128)}, f32[1544,128]{1,0:T(8,128)S(1)}, u32[]{:S(2)}, u32[]{:S(2)}) collective-permute-start(f32[1544,128]{1,0:T(8,128)} %slice.318), channel_id=1, source_target_pairs={{1,0},{2,1},{3,2},{4,3},{5,4},{6,5},{7,6},{8,7},{9,8},{10,9},{11,1... | collective-permute-start | bytes 2371592 | tf_op jit(solution)/shard_map/ppermute | solution.py:249
  13.9 2.1 %slice.319 = f32[1536,128]{1,0:T(8,128)} slice(f32[4096,128]{1,0:T(8,128)} %rec_ref.1), slice={[2560:4096], [0:128]} | slice | bytes 1572864 | tf_op jit(solution)/shard_map/slice | solution.py:263
  16.0 1.9 %collective-permute-start.1 = (f32[1536,128]{1,0:T(8,128)}, f32[1536,128]{1,0:T(8,128)}, u32[]{:S(2)}, u32[]{:S(2)}) collective-permute-start(f32[1536,128]{1,0:T(8,128)} %slice.319), channel_id=1, source_target_pairs={{0,1},{1,2},{2,3},{3,4},{4,5},{5,6},{6,7},{7,8},{8,9},{9,10},{10,1... | collective-permute-start | bytes 2359304 | tf_op jit(solution)/shard_map/ppermute | solution.py:249
  17.9 0.1 add_convert_fusion.edge_ref
  18.0 0.0 copy-done
  18.0 6.3 %local_products.1 = (f32[26,128,128]{2,1,0:T(8,128)S(1)}, bf16[4096,512]{1,0:T(8,128)(2,1)}) custom-call(s32[2]{0:T(128)S(1)} %add_convert_fusion.edge_ref, f32[4096,128]{1,0:T(8,128)S(1)} %copy-done), custom_call_target="tpu_custom_call" | custom-call | flops 4000000000 | bytes 8388608 | tf_op jit(solution)/shard_map/local_products/pallas_call | solution.py:267
  24.3 17.0 %collective-permute-done.1.up_ref = f32[1536,128]{1,0:T(8,128)} collective-permute-done((f32[1536,128]{1,0:T(8,128)}, f32[1536,128]{1,0:T(8,128)}, u32[]{:S(2)}, u32[]{:S(2)}) %collective-permute-start.1) | collective-permute-done | bytes 786464 | tf_op jit(solution)/shard_map/ppermute | solution.py:249
  41.3 0.0 collective-permute-done.down_ref
  41.3 5.2 %halo_products.1 = f32[26,128,128]{2,1,0:T(8,128)S(1)} custom-call(s32[2]{0:T(128)S(1)} %add_convert_fusion.edge_ref, f32[26,128,128]{2,1,0:T(8,128)S(1)} %get-tuple-element.4.acc_ref, bf16[4096,512]{1,0:T(8,128)(2,1)} %get-tuple-element.5.split_ref, f32[1544,128]{1,0:T(8,128)S(1)} %collective-permute-done.down_ref, f32[1536,128]{1,0:T(8,128)} %collective-permute-done.1.up_ref), custom_call_target="tpu_custom_call" | custom-call | flops 3000000000 | bytes 9437184 | tf_op jit(solution)/shard_map/halo_products/pallas_call | solution.py:277
  46.7 87.7 %all-reduce.2 = (f32[32,128]{1,0:T(8,128)S(1)}, f32[32,128]{1,0:T(8,128)S(1)}, f32[32,128]{1,0:T(8,128)S(1)}, f32[32,128]{1,0:T(8,128)S(1)}, f32[32,128]{1,0:T(8...) all-reduce(f32[32,128]{1,0:T(8,128)S(1)} %get-tuple-element.213, ...), channel_id=1, replica_groups=mesh['grp'=8,'span'=32] {'grp','span'}, use_global_device_ids=true, to_apply=%region_0.0 | all-reduce | flops 425984 | bytes 3407872 | tf_op jit(solution)/shard_map/psum | solution.py:253
  135.7 25.3 %factor_and_solve.1 = (f32[512,512]{1,0:T(8,128)}, f32[512,512]{1,0:T(8,128)}) custom-call(f32[26,128,128]{2,1,0:T(8,128)S(1)} %bitcast.4), custom_call_target="tpu_custom_call" | custom-call | tf_op jit(solution)/shard_map/factor_and_solve/pallas_call | solution.py:296
  (110 shorter events, 0.5 us)
Async XLA Ops:
  0.6 17.4 %copy-start = (f32[4096,128]{1,0:T(8,128)S(1)}, f32[4096,128]{1,0:T(8,128)}, u32[]{:S(2)}) copy-start(f32[4096,128]{1,0:T(8,128)} %rec_ref.1) | copy-start | bytes 6291460
  2.9 38.5 %collective-permute-start = (f32[1544,128]{1,0:T(8,128)}, f32[1544,128]{1,0:T(8,128)S(1)}, u32[]{:S(2)}, u32[]{:S(2)}) collective-permute-start(f32[1544,128]{1,0:T(8,128)} %slice.318), channel_id=1, source_target_pairs={{1,0},{2,1},{3,2},{4,3},{5,4},{6,5},{7,6},{8,7},{9,8},{10,9},{11,1... | collective-permute-start | bytes 2371592 | tf_op jit(solution)/shard_map/ppermute | solution.py:249
  16.0 25.3 %collective-permute-start.1 = (f32[1536,128]{1,0:T(8,128)}, f32[1536,128]{1,0:T(8,128)}, u32[]{:S(2)}, u32[]{:S(2)}) collective-permute-start(f32[1536,128]{1,0:T(8,128)} %slice.319), channel_id=1, source_target_pairs={{0,1},{1,2},{2,3},{3,4},{4,5},{5,6},{6,7},{7,8},{8,9},{9,10},{10,1... | collective-permute-start | bytes 2359304 | tf_op jit(solution)/shard_map/ppermute | solution.py:249

commit v2 on v1

--- a/solution.py
+++ b/solution.py
@@ -21,6 +21,8 @@
 GRAM = {pair: index for index, pair in enumerate(PAIRS)}
 CROSS = {(i, j): len(PAIRS) + LAGS * i + j for i in range(LAGS) for j in range(LAGS)}
 BLOCKS = len(GRAM) + len(CROSS)
+SIDE = BLOCKS // 2
+CHIPS_X = 4
 
 
 def exact(left, right, dims):
@@ -114,7 +116,27 @@
                 out_ref[CROSS[i, j]] -= exact(c, a, outer) if i >= j else exact(a, c, outer)
 
 
-def halo_kernel(edge_ref, acc_ref, split_ref, down_ref, up_ref, out_ref, below, above):
+def carve_kernel(rec_ref, head_ref, rear_ref, sems):
+    head, rear = head_ref.shape[0], rear_ref.shape[0]
+    copies = [
+        pltpu.make_async_copy(rec_ref.at[:head], head_ref, sems.at[0]),
+        pltpu.make_async_copy(rec_ref.at[rec_ref.shape[0] - rear :], rear_ref, sems.at[1]),
+    ]
+    for copy in copies:
+        copy.start()
+    for copy in copies:
+        copy.wait()
+
+
+def fan_kernel(in_ref, out_ref):
+    value = in_ref[0]
+    for k in range(1, in_ref.shape[0]):
+        value = value + in_ref[k]
+    for k in range(out_ref.shape[0]):
+        out_ref[k] = value
+
+
+def halo_kernel(edge_ref, acc_ref, split_ref, down_ref, up_ref, keep_ref, give_ref, below, above, stage):
     below[:, : 2 * N] = parts(down_ref[:SPAN, :])
     below[:, 2 * N :] = parts(down_ref[1 : SPAN + 1, :])
     above[:, : 2 * N] = parts(up_ref[...])
@@ -135,13 +157,18 @@
             (above[:HALF, :], own_rows(DELAY + HALF, HALF)),
         ],
     }
+    core = edge_ref[2]
+
+    def put(index, value):
+        stage[(index // SIDE) ^ core, index % SIDE] = value
+
     lastrow = lax.broadcasted_iota(jnp.int32, (16, N), 0) == 15
     entering = parts(jnp.where(lastrow, jnp.broadcast_to(down_ref[0:1, :], (16, N)), 0.0))
     count = LAGS * DELAY
     fix = fold(rows_product(entering, split_ref[count - 16 : count, : 2 * N]))
     for i in range(LAGS):
-        out_ref[GRAM[i, i]] = acc_ref[GRAM[i, i]]
-        out_ref[CROSS[i, i]] = acc_ref[CROSS[i, i]] + fix
+        put(GRAM[i, i], acc_ref[GRAM[i, i]])
+        put(CROSS[i, i], acc_ref[CROSS[i, i]] + fix)
     for d in range(1, LAGS):
         stop = (LAGS - d) * DELAY
         same = None
@@ -154,9 +181,11 @@
             ahead = ahead + a
         for i in range(LAGS - d):
             j = i + d
-            out_ref[GRAM[i, j]] = acc_ref[GRAM[i, j]] + same
-            out_ref[CROSS[j, i]] = acc_ref[CROSS[j, i]] + back
-            out_ref[CROSS[i, j]] = acc_ref[CROSS[i, j]] + ahead
+            put(GRAM[i, j], acc_ref[GRAM[i, j]] + same)
+            put(CROSS[j, i], acc_ref[CROSS[j, i]] + back)
+            put(CROSS[i, j], acc_ref[CROSS[i, j]] + ahead)
+    keep_ref[...] = stage[0]
+    give_ref[...] = stage[1]
 
 
 def lanes(value, j):
@@ -202,12 +231,18 @@
     return jnp.concatenate(uppers, 0), jnp.concatenate(inverses, 0)
 
 
-def tail_kernel(scale, sum_ref, tri_ref, op_ref, work, right, inv):
+def tail_kernel(scale, edge_ref, mine_ref, other_ref, tri_ref, op_ref, work, right, inv):
+    core = edge_ref[2]
+
+    def summed(index):
+        a, b = mine_ref[index % SIDE], other_ref[index % SIDE]
+        return jnp.where(core == index // SIDE, a, b)
+
     for i in range(LAGS):
         for j in range(LAGS):
             if j >= i:
-                work[i, :, j * N : (j + 1) * N] = sum_ref[GRAM[i, j]] * scale
-            block = sum_ref[CROSS[i, j]]
+                work[i, :, j * N : (j + 1) * N] = summed(GRAM[i, j]) * scale
+            block = summed(CROSS[i, j])
             work[i, :, COLS + j * N : COLS + (j + 1) * N] = (block.T if i >= j else block) * scale
     rows = lax.broadcasted_iota(jnp.int32, (N, N), 0)
     eye = jnp.where(rows == lax.broadcasted_iota(jnp.int32, (N, N), 1), 1.0, 0.0).astype(jnp.float32)
@@ -249,24 +284,72 @@
     return lax.ppermute(value, AXES, [(source, source + steps) for source in range(leading, last)])
 
 
-def spread_sum(value):
-    pieces = lax.psum(tuple(value[r : r + 32] for r in range(0, value.shape[0], 32)), AXES)
-    return jnp.concatenate(pieces, 0)
-
-
-def averaged_blocks(record):
+def trade(value, groups):
+    if len(groups[0]) == 1:
+        return value
+    return lax.all_to_all(value, AXES, 0, 0, axis_index_groups=groups)
+
+
+def fan(value, copies):
+    return pl.pallas_call(
+        fan_kernel,
+        out_shape=jax.ShapeDtypeStruct((copies,) + value.shape[1:], jnp.float32),
+        in_specs=[pl.BlockSpec(memory_space=pltpu.VMEM)],
+        out_specs=pl.BlockSpec(memory_space=pltpu.VMEM),
+        compiler_params=pltpu.CompilerParams(vmem_limit_bytes=VMEM_LIMIT),
+        name="add_and_repeat",
+    )(value)
+
+
+def across_cores(value):
+    count = lax.axis_size("grp")
+    return lax.ppermute(value, "grp", [(source, source ^ 1) for source in range(count)])
+
+
+def spread_sum(keep, give):
+    rows, depth = lax.axis_size("grp") // 2, lax.axis_size("span") // CHIPS_X
+
+    def device(y, core, z, x):
+        return ((y * 2 + core) * depth + z) * CHIPS_X + x
+
+    planes = [
+        [device(y, core, z, x) for y in range(rows) for x in range(CHIPS_X)] for core in range(2) for z in range(depth)
+    ]
+    columns = [
+        [device(y, core, z, x) for z in range(depth)]
+        for y in range(rows)
+        for core in range(2)
+        for x in range(CHIPS_X)
+    ]
+    plane = rows * CHIPS_X
+    half = keep + across_cores(give)
+    shares = trade(half.reshape(plane, SIDE * N // plane, N), planes)
+    shares = trade(fan(shares, depth), columns)
+    mine = trade(fan(shares, plane), planes).reshape(SIDE, N, N)
+    return mine, across_cores(mine)
+
+
+def averaged_blocks(record, edge):
     count = record.shape[0]
-    devices = lax.axis_size(AXES)
-    index = lax.axis_index(AXES)
-    edge = jnp.stack([index == 0, index == devices - 1]).astype(jnp.int32)
-    down = shifted(record[: SPAN + 8], -1)
-    up = shifted(record[count - SPAN :], 1)
     smem, vmem = pl.BlockSpec(memory_space=pltpu.SMEM), pl.BlockSpec(memory_space=pltpu.VMEM)
+    anywhere = pl.BlockSpec(memory_space=pl.ANY)
     params = pltpu.CompilerParams(vmem_limit_bytes=VMEM_LIMIT)
-    block = jax.ShapeDtypeStruct((BLOCKS, N, N), jnp.float32)
+    head, rear = pl.pallas_call(
+        carve_kernel,
+        out_shape=[jax.ShapeDtypeStruct((SPAN + 8, N), jnp.float32), jax.ShapeDtypeStruct((SPAN, N), jnp.float32)],
+        in_specs=[anywhere],
+        out_specs=[vmem, vmem],
+        scratch_shapes=[pltpu.SemaphoreType.DMA((2,))],
+        compiler_params=params,
+        name="carve",
+    )(record)
+    down, up = shifted(head, -1), shifted(rear, 1)
     local, split = pl.pallas_call(
         local_kernel,
-        out_shape=[block, jax.ShapeDtypeStruct((count, 4 * N), jnp.bfloat16)],
+        out_shape=[
+            jax.ShapeDtypeStruct((BLOCKS, N, N), jnp.float32),
+            jax.ShapeDtypeStruct((count, 4 * N), jnp.bfloat16),
+        ],
         in_specs=[smem, vmem],
         out_specs=[vmem, vmem],
         scratch_shapes=[pltpu.VMEM((LAGS * LAGS, N, N), jnp.float32)] * 3,
@@ -274,29 +357,33 @@
         cost_estimate=pl.CostEstimate(flops=4 * 10**9, bytes_accessed=8 * 2**20, transcendentals=0),
         name="local_products",
     )(edge, record)
-    summed = pl.pallas_call(
+    side = jax.ShapeDtypeStruct((SIDE, N, N), jnp.float32)
+    keep, give = pl.pallas_call(
         halo_kernel,
-        out_shape=block,
+        out_shape=[side, side],
         in_specs=[smem, vmem, vmem, vmem, vmem],
-        out_specs=vmem,
-        scratch_shapes=[pltpu.VMEM((SPAN, 4 * N), jnp.bfloat16)] * 2,
+        out_specs=[vmem, vmem],
+        scratch_shapes=[pltpu.VMEM((SPAN, 4 * N), jnp.bfloat16)] * 2 + [pltpu.VMEM((2, SIDE, N, N), jnp.float32)],
         compiler_params=params,
         cost_estimate=pl.CostEstimate(flops=3 * 10**9, bytes_accessed=9 * 2**20, transcendentals=0),
         name="halo_products",
     )(edge, local, split, down, up)
-    return spread_sum(summed.reshape(BLOCKS * N, N)).reshape(BLOCKS, N, N)
+    return spread_sum(keep, give)
 
 
 def on_device(record):
-    last_row = record.shape[0] * lax.axis_size(AXES) - (LAGS - 1) * DELAY - 1
-    total = averaged_blocks(record)
-    vmem = pl.BlockSpec(memory_space=pltpu.VMEM)
+    devices = lax.axis_size(AXES)
+    last_row = record.shape[0] * devices - (LAGS - 1) * DELAY - 1
+    index = lax.axis_index(AXES)
+    edge = jnp.stack([index == 0, index == devices - 1, lax.axis_index("grp") % 2]).astype(jnp.int32)
+    mine, other = averaged_blocks(record, edge)
+    smem, vmem = pl.BlockSpec(memory_space=pltpu.SMEM), pl.BlockSpec(memory_space=pltpu.VMEM)
     square = jax.ShapeDtypeStruct((COLS, COLS), jnp.float32)
     return tuple(
         pl.pallas_call(
             functools.partial(tail_kernel, 1.0 / last_row),
             out_shape=[square, square],
-            in_specs=[vmem],
+            in_specs=[smem, vmem, vmem],
             out_specs=[vmem, vmem],
             scratch_shapes=[
                 pltpu.VMEM((LAGS, N, 2 * COLS), jnp.float32),
@@ -305,7 +392,7 @@
             ],
             compiler_params=pltpu.CompilerParams(vmem_limit_bytes=VMEM_LIMIT),
             name="factor_and_solve",
-        )(total)
+        )(edge, mine, other)
     )
 
 

time: 161 us -> 131 us (0.81)
  blocking collectives: 87.7 us -> 50.7 us
  waiting for transfers between devices: 17 us -> 21.4 us
  starting transfers between devices: 13 us -> 16.8 us
  local copies, waits for them, and re-layouts: 4.82 us -> 1.59 us
  Pallas kernels: 36.8 us -> 38.9 us
    psum x1 -> x0, blocking collectives: 87.7 us -> none  [spread_sum(): lax.psum(tuple((value[r:r + 32] for r in range(0, value.shape[0], 32))),...]
    all_to_all x0 -> x3, blocking collectives: none -> 50.7 us  [trade(): return lax.all_to_all(value, AXES, 0, 0, axis_index_groups=groups)]
    slice x8 -> x0, local copies, waits for them, and re-layouts: 4.43 us -> none  [the longest x1 2.22 us: averaged_blocks(): down = shifted(record[:SPAN + 8], -1)]
    ppermute x0 -> x2, waiting for transfers between devices: none -> 4.37 us  [across_cores(): lax.ppermute(value, 'grp', [(source, source ^ 1) for source in range(coun...]
    ppermute x0 -> x2, starting transfers between devices: none -> 3.77 us  [across_cores(): lax.ppermute(value, 'grp', [(source, source ^ 1) for source in range(coun...]
    pallas_call x2 -> x5, Pallas kernels: 11.5 us -> 13.1 us  [the longest x1 6.27 us: averaged_blocks(): pl.pallas_call(local_kernel, out_shape=[jax.ShapeDtypeStruct((BLOCKS, N,...]
  transfers between devices with their start and end apart: 2 -> 4, of which waited for: 1 -> 3; matrix products, arithmetic and copies ran while one was open for 1% -> 0% of each run, Pallas kernels for 4% -> 5%
where the time goes in v2:
time: 131 us; the launch traced here: 130 us
  blocking collectives  50.7 us (39%)
  Pallas kernels  38.9 us (30%)
  waiting for transfers between devices  21.4 us (16%)
  starting transfers between devices  16.8 us (13%)
  local copies, waits for them, and re-layouts  1.59 us (1%)
    all_to_all x3, blocking collectives, trade(): return lax.all_to_all(value, AXES, 0, 0, axis_index_groups=groups)  50.7 us
    pallas_call x1, Pallas kernels, on_device(): pl.pallas_call(functools.partial(tail_kernel, 1.0 / last_row), out_shape=...  25.8 us
    ppermute x2, waiting for transfers between devices, shifted(): lax.ppermute(value, AXES, [(source, source + steps) for source in range(l...  17 us
    ppermute x2, starting transfers between devices, shifted(): lax.ppermute(value, AXES, [(source, source + steps) for source in range(l...  13 us
    pallas_call x1, Pallas kernels, averaged_blocks(): pl.pallas_call(local_kernel, out_shape=[jax.ShapeDtypeStruct((BLOCKS, N,...  6.27 us
    pallas_call x1, Pallas kernels, averaged_blocks(): pl.pallas_call(halo_kernel, out_shape=[side, side], in_specs=[smem, vmem,...  5.44 us
    ppermute x2, waiting for transfers between devices, across_cores(): lax.ppermute(value, 'grp', [(source, source ^ 1) for source in range(coun...  4.37 us
    ppermute x2, starting transfers between devices, across_cores(): lax.ppermute(value, 'grp', [(source, source ^ 1) for source in range(coun...  3.77 us
  transfers between devices with their start and end apart: 4, of which 3 were waited for; matrix products, arithmetic and copies ran while one was open for 0% of the time, Pallas kernels for 5%

profile of v2, /device:TPU:1, one launch (start us, length us, event | category | flops | bytes accessed | tf_op | source)
XLA Modules:
  0.0 130.3 jit_solution(18140738700534274739)
XLA Ops:
  0.6 0.0 copy-start
  0.6 1.6 %copy-done = f32[4096,128]{1,0:T(8,128)S(1)} copy-done((f32[4096,128]{1,0:T(8,128)S(1)}, f32[4096,128]{1,0:T(8,128)}, u32[]{:S(2)}) %copy-start) | copy-done | bytes 2097176
  2.2 0.0 copy-start.1
  2.2 1.3 carve.1
  3.5 11.1 %collective-permute-start = (f32[1544,128]{1,0:T(8,128)}, f32[1544,128]{1,0:T(8,128)S(1)}, u32[]{:S(2)}, u32[]{:S(2)}) collective-permute-start(f32[1544,128]{1,0:T(8,128)} %get-tuple-element.10), channel_id=1, source_target_pairs={{1,0},{2,1},{3,2},{4,3},{5,4},{6,5},{7,6},{8,7},{9,8},{10,9},{11,1... | collective-permute-start | bytes 2371592 | tf_op jit(solution)/shard_map/ppermute | solution.py:284
  14.6 1.9 %collective-permute-start.1 = (f32[1536,128]{1,0:T(8,128)}, f32[1536,128]{1,0:T(8,128)}, u32[]{:S(2)}, u32[]{:S(2)}) collective-permute-start(f32[1536,128]{1,0:T(8,128)} %get-tuple-element.11), channel_id=1, source_target_pairs={{0,1},{1,2},{2,3},{3,4},{4,5},{5,6},{6,7},{7,8},{8,9},{9,10},{10,1... | collective-permute-start | bytes 2359304 | tf_op jit(solution)/shard_map/ppermute | solution.py:284
  16.5 0.1 pad_add_fusion.edge_ref
  16.6 0.0 copy-done.1
  16.6 6.3 %local_products.1 = (f32[26,128,128]{2,1,0:T(8,128)S(1)}, bf16[4096,512]{1,0:T(8,128)(2,1)}) custom-call(s32[3]{0:T(128)S(1)} %pad_add_fusion.edge_ref, f32[4096,128]{1,0:T(8,128)S(1)} %copy-done.1), custom_call_target="tpu_custom_call" | custom-call | flops 4000000000 | bytes 8388608 | tf_op jit(solution)/shard_map/local_products/pallas_call | solution.py:347
  22.9 17.0 %collective-permute-done.1.up_ref = f32[1536,128]{1,0:T(8,128)} collective-permute-done((f32[1536,128]{1,0:T(8,128)}, f32[1536,128]{1,0:T(8,128)}, u32[]{:S(2)}, u32[]{:S(2)}) %collective-permute-start.1) | collective-permute-done | bytes 786464 | tf_op jit(solution)/shard_map/ppermute | solution.py:284
  39.9 0.0 collective-permute-done.down_ref
  39.9 5.4 %halo_products.1 = (f32[13,128,128]{2,1,0:T(8,128)S(1)}, f32[13,128,128]{2,1,0:T(8,128)S(1)}) custom-call(s32[3]{0:T(128)S(1)} %pad_add_fusion.edge_ref, f32[26,128,128]{2,1,0:T(8,128)S(1)} %get-tuple-element.8.acc_ref, bf16[4096,512]{1,0:T(8,128)(2,1)} %get-tuple-element.9.split_ref, f32[1544,128]{1,0:T(8,128)S(1)} %collective-permute-done.down_ref, ...), custom_call_target="tpu_custom_call" | custom-call | flops 3000000000 | bytes 9437184 | tf_op jit(solution)/shard_map/halo_products/pallas_call | solution.py:361
  45.4 0.1 collective-permute-start.2
  45.5 2.4 %collective-permute-done.2 = f32[13,128,128]{2,1,0:T(8,128)S(1)} collective-permute-done((f32[13,128,128]{2,1,0:T(8,128)S(1)}, f32[13,128,128]{2,1,0:T(8,128)S(1)}, u32[]{:S(2)}, u32[]{:S(2)}) %collective-permute-start.2) | collective-permute-done | bytes 852000 | tf_op jit(solution)/shard_map/ppermute | solution.py:306
  47.8 0.1 add.12
  47.9 19.0 %all_to_all.15.in_ref = f32[16,104,128]{2,1,0:T(8,128)S(1)} all-to-all(f32[16,104,128]{2,1,0:T(8,128)S(1)} %bitcast.7), channel_id=1, replica_groups={{0,1,2,3,64,65,66,67,128,129,130,131,192,193,194,195},{4,5,6,7,68,69,70..., dimensions={0} | all-to-all | bytes 1703936 | tf_op jit(solution)/shard_map/all_to_all | solution.py:290
  66.9 0.1 add_and_repeat.2
  67.0 16.1 %all_to_all.16.in_ref = f32[8,104,128]{2,1,0:T(8,128)S(1)} all-to-all(f32[8,104,128]{2,1,0:T(8,128)S(1)} %add_and_repeat.2), channel_id=1, replica_groups={{0,4,8,12,16,20,24,28},{1,5,9,13,17,21,25,29},{2,6,10,14,18,22,26,30},{..., dimensions={0} | all-to-all | bytes 851968 | tf_op jit(solution)/shard_map/all_to_all | solution.py:290
  83.1 0.1 add_and_repeat.3
  83.2 15.6 %all_to_all.17 = f32[16,104,128]{2,1,0:T(8,128)S(1)} all-to-all(f32[16,104,128]{2,1,0:T(8,128)S(1)} %add_and_repeat.3), channel_id=1, replica_groups={{0,1,2,3,64,65,66,67,128,129,130,131,192,193,194,195},{4,5,6,7,68,69,70..., dimensions={0} | all-to-all | bytes 1703936 | tf_op jit(solution)/shard_map/all_to_all | solution.py:290
  98.8 3.7 %collective-permute-start.3 = (f32[13,128,128]{2,1,0:T(8,128)S(1)}, f32[13,128,128]{2,1,0:T(8,128)S(1)}, u32[]{:S(2)}, u32[]{:S(2)}) collective-permute-start(f32[13,128,128]{2,1,0:T(8,128)S(1)} %bitcast.5), channel_id=1, source_target_pairs={{0,32},{32,0},{64,96},{96,64},{128,160},{160,128},{192,224},{224,1... | collective-permute-start | bytes 2555912 | tf_op jit(solution)/shard_map/ppermute | solution.py:306
  102.5 2.0 %collective-permute-done.3.other_ref = f32[13,128,128]{2,1,0:T(8,128)S(1)} collective-permute-done((f32[13,128,128]{2,1,0:T(8,128)S(1)}, f32[13,128,128]{2,1,0:T(8,128)S(1)}, u32[]{:S(2)}, u32[]{:S(2)}) %collective-permute-start.3) | collective-permute-done | bytes 852000 | tf_op jit(solution)/shard_map/ppermute | solution.py:306
  104.5 25.8 %factor_and_solve.1 = (f32[512,512]{1,0:T(8,128)}, f32[512,512]{1,0:T(8,128)}) custom-call(s32[3]{0:T(128)S(1)} %pad_add_fusion.edge_ref, f32[13,128,128]{2,1,0:T(8,128)S(1)} %bitcast.6, f32[13,128,128]{2,1,0:T(8,128)S(1)} %collective-permute-done.3.other_ref), custom_call_target="tpu_custom_call" | custom-call | tf_op jit(solution)/shard_map/factor_and_solve/pallas_call | solution.py:383
Async XLA Ops:
  0.6 1.6 %copy-start = (f32[4096,128]{1,0:T(8,128)S(1)}, f32[4096,128]{1,0:T(8,128)}, u32[]{:S(2)}) copy-start(f32[4096,128]{1,0:T(8,128)} %rec_ref.3) | copy-start | bytes 6291460
  2.2 14.4 %copy-start.1 = (f32[4096,128]{1,0:T(8,128)S(1)}, f32[4096,128]{1,0:T(8,128)}, u32[]{:S(2)}) copy-start(f32[4096,128]{1,0:T(8,128)} %rec_ref.3) | copy-start | bytes 6291460
  3.5 36.4 %collective-permute-start = (f32[1544,128]{1,0:T(8,128)}, f32[1544,128]{1,0:T(8,128)S(1)}, u32[]{:S(2)}, u32[]{:S(2)}) collective-permute-start(f32[1544,128]{1,0:T(8,128)} %get-tuple-element.10), channel_id=1, source_target_pairs={{1,0},{2,1},{3,2},{4,3},{5,4},{6,5},{7,6},{8,7},{9,8},{10,9},{11,1... | collective-permute-start | bytes 2371592 | tf_op jit(solution)/shard_map/ppermute | solution.py:284
  14.6 25.3 %collective-permute-start.1 = (f32[1536,128]{1,0:T(8,128)}, f32[1536,128]{1,0:T(8,128)}, u32[]{:S(2)}, u32[]{:S(2)}) collective-permute-start(f32[1536,128]{1,0:T(8,128)} %get-tuple-element.11), channel_id=1, source_target_pairs={{0,1},{1,2},{2,3},{3,4},{4,5},{5,6},{6,7},{7,8},{8,9},{9,10},{10,1... | collective-permute-start | bytes 2359304 | tf_op jit(solution)/shard_map/ppermute | solution.py:284
  45.4 2.5 %collective-permute-start.2 = (f32[13,128,128]{2,1,0:T(8,128)S(1)}, f32[13,128,128]{2,1,0:T(8,128)S(1)}, u32[]{:S(2)}, u32[]{:S(2)}) collective-permute-start(f32[13,128,128]{2,1,0:T(8,128)S(1)} %get-tuple-element.13), channel_id=1, source_target_pairs={{0,32},{32,0},{64,96},{96,64},{128,160},{160,128},{192,224},{224,1... | collective-permute-start | bytes 2555912 | tf_op jit(solution)/shard_map/ppermute | solution.py:306
  98.8 5.7 %collective-permute-start.3 = (f32[13,128,128]{2,1,0:T(8,128)S(1)}, f32[13,128,128]{2,1,0:T(8,128)S(1)}, u32[]{:S(2)}, u32[]{:S(2)}) collective-permute-start(f32[13,128,128]{2,1,0:T(8,128)S(1)} %bitcast.5), channel_id=1, source_target_pairs={{0,32},{32,0},{64,96},{96,64},{128,160},{160,128},{192,224},{224,1... | collective-permute-start | bytes 2555912 | tf_op jit(solution)/shard_map/ppermute | solution.py:306

commit v3 on v2

--- a/solution.py
+++ b/solution.py
@@ -21,8 +21,9 @@
 GRAM = {pair: index for index, pair in enumerate(PAIRS)}
 CROSS = {(i, j): len(PAIRS) + LAGS * i + j for i in range(LAGS) for j in range(LAGS)}
 BLOCKS = len(GRAM) + len(CROSS)
-SIDE = BLOCKS // 2
+GRAM_SIDE, CROSS_SIDE = len(GRAM) // 2, len(CROSS) // 2
 CHIPS_X = 4
+GROUP = 4
 
 
 def exact(left, right, dims):
@@ -128,15 +129,19 @@
         copy.wait()
 
 
-def fan_kernel(in_ref, out_ref):
+def fan_kernel(in_ref, *out_refs):
     value = in_ref[0]
     for k in range(1, in_ref.shape[0]):
         value = value + in_ref[k]
-    for k in range(out_ref.shape[0]):
-        out_ref[k] = value
-
-
-def halo_kernel(edge_ref, acc_ref, split_ref, down_ref, up_ref, keep_ref, give_ref, below, above, stage):
+    start = 0
+    for out_ref in out_refs:
+        size = out_ref.shape[1]
+        for k in range(out_ref.shape[0]):
+            out_ref[k] = value[start : start + size]
+        start += size
+
+
+def halo_kernel(edge_ref, acc_ref, split_ref, down_ref, up_ref, keep_ref, give_ref, below, above, gram, cross):
     below[:, : 2 * N] = parts(down_ref[:SPAN, :])
     below[:, 2 * N :] = parts(down_ref[1 : SPAN + 1, :])
     above[:, : 2 * N] = parts(up_ref[...])
@@ -160,7 +165,13 @@
     core = edge_ref[2]
 
     def put(index, value):
-        stage[(index // SIDE) ^ core, index % SIDE] = value
+        if index < len(GRAM):
+            index, row = index // GRAM_SIDE, index % GRAM_SIDE * N
+            gram[index ^ core, row : row + N] = value
+        else:
+            index -= len(GRAM)
+            index, row = index // CROSS_SIDE, index % CROSS_SIDE * N
+            cross[index ^ core, row : row + N] = value
 
     lastrow = lax.broadcasted_iota(jnp.int32, (16, N), 0) == 15
     entering = parts(jnp.where(lastrow, jnp.broadcast_to(down_ref[0:1, :], (16, N)), 0.0))
@@ -184,8 +195,12 @@
             put(GRAM[i, j], acc_ref[GRAM[i, j]] + same)
             put(CROSS[j, i], acc_ref[CROSS[j, i]] + back)
             put(CROSS[i, j], acc_ref[CROSS[i, j]] + ahead)
-    keep_ref[...] = stage[0]
-    give_ref[...] = stage[1]
+    members = keep_ref.shape[0]
+    few, many = GRAM_SIDE * N // members, CROSS_SIDE * N // members
+    for side, ref in enumerate((keep_ref, give_ref)):
+        for m in range(members):
+            ref[m, :few] = gram[side, m * few : (m + 1) * few]
+            ref[m, few:] = cross[side, m * many : (m + 1) * many]
 
 
 def lanes(value, j):
@@ -196,86 +211,124 @@
     return jnp.broadcast_to(value[t : t + 1, :], (n, N))
 
 
-def factor(rest, inverse):
+def three(value):
+    high = value.astype(jnp.bfloat16)
+    rest = value - high.astype(jnp.float32)
+    mid = rest.astype(jnp.bfloat16)
+    return high, mid, (rest - mid.astype(jnp.float32)).astype(jnp.bfloat16)
+
+
+def stacked(left, right, dim):
+    (a, b, c), (x, y, z) = three(left), three(right)
+    return lax.dot_general(
+        jnp.concatenate([a, a, b, a, c, b], dim),
+        jnp.concatenate([x, y, x, z, x, y], 0),
+        (((dim,), (0,)), ((), ())),
+        preferred_element_type=jnp.float32,
+    )
+
+
+def factor(matrix):
     sub = lax.broadcasted_iota(jnp.int32, (8, N), 0)
     lane = lax.broadcasted_iota(jnp.int32, (8, N), 1)
+    rows = [matrix[r : r + 8] for r in range(0, N, 8)]
     uppers, inverses = [], []
-    for k in range(N // 8):
-        n = rest.shape[0] - 8
-        top, top_inverse = rest[:8], inverse[:8]
-        cols = [lanes(top, 8 * k + t) for t in range(8)]
-        if n:
-            rest, inverse = rest[8:], inverse[8:]
-            below = [lanes(rest, 8 * k + t) for t in range(8)]
+    for k in range(len(rows)):
+        first = 8 * k
+        old, inside = lane < first + 8, (lane >= first) & (lane < first + 8)
+        top = rows[k]
+        grown = jnp.where(lane < first, top, 0.0) + jnp.where(lane == sub + first, 1.0, 0.0)
+        cols = [lanes(top, first + t) for t in range(8)]
+        others = list(range(k + 1, k - k % GROUP + GROUP))
+        below = {v: [lanes(rows[v], first + t) for t in range(8)] for v in others}
+        for v in others:
+            rows[v] = jnp.where(inside, 0.0, rows[v])
         pivots = jnp.zeros((8, N), jnp.float32)
         for t in range(8):
             pivot = line(cols[t], t, 8)
             recip = 1.0 / pivot
             mult = jnp.where(sub > t, cols[t] * recip, 0.0)
-            if n:
-                mult_below = below[t] * jnp.broadcast_to(recip[:1], (n, N))
-            for u in range(t + 1, 8):
-                entry = cols[u][t : t + 1, :]
-                if n:
-                    below[u] = below[u] - mult_below * jnp.broadcast_to(entry, (n, N))
-                cols[u] = cols[u] - mult * jnp.broadcast_to(entry, (8, N))
+            entries = [line(cols[u], t, 8) for u in range(t + 1, 8)]
+            top_line, grown_line = line(top, t, 8), line(grown, t, 8)
+            for u, entry in zip(range(t + 1, 8), entries):
+                cols[u] = cols[u] - mult * entry
             pivots = jnp.where(sub == t, pivot, pivots)
-            if n:
-                rest = rest - mult_below * line(top, t, n)
-                inverse = inverse - mult_below * line(top_inverse, t, n)
-            top = top - mult * line(top, t, 8)
-            top_inverse = top_inverse - mult * line(top_inverse, t, 8)
+            if others:
+                both = jnp.where(old, grown_line, top_line)
+            for v in others:
+                mult_below = below[v][t] * recip
+                for u, entry in zip(range(t + 1, 8), entries):
+                    below[v][u] = below[v][u] - mult_below * entry
+                rows[v] = rows[v] - mult_below * both
+            top = top - mult * top_line
+            grown = grown - mult * grown_line
         root = lax.rsqrt(pivots)
-        uppers.append(jnp.where(lane >= sub + 8 * k, top * root, 0.0))
-        inverses.append(top_inverse * root)
+        uppers.append(jnp.where(lane >= sub + first, top * root, 0.0))
+        inverses.append(grown * root)
+        end = k + 1
+        if end % GROUP == 0 and end < len(rows):
+            upper = jnp.concatenate(uppers[-GROUP:], 0)
+            columns = lax.broadcasted_iota(jnp.int32, upper.shape, 1)
+            done = jnp.where(columns < 8 * end, jnp.concatenate(inverses[-GROUP:], 0), upper)
+            update = stacked(upper, done, 0)
+            grouped = (lane >= 8 * (end - GROUP)) & (lane < 8 * end)
+            for v in range(end, len(rows)):
+                rows[v] = jnp.where(grouped, 0.0, rows[v]) - update[8 * v : 8 * v + 8]
     return jnp.concatenate(uppers, 0), jnp.concatenate(inverses, 0)
 
 
-def tail_kernel(scale, edge_ref, mine_ref, other_ref, tri_ref, op_ref, work, right, inv):
-    core = edge_ref[2]
-
-    def summed(index):
-        a, b = mine_ref[index % SIDE], other_ref[index % SIDE]
-        return jnp.where(core == index // SIDE, a, b)
-
-    for i in range(LAGS):
-        for j in range(LAGS):
-            if j >= i:
-                work[i, :, j * N : (j + 1) * N] = summed(GRAM[i, j]) * scale
-            block = summed(CROSS[i, j])
-            work[i, :, COLS + j * N : COLS + (j + 1) * N] = (block.T if i >= j else block) * scale
-    rows = lax.broadcasted_iota(jnp.int32, (N, N), 0)
-    eye = jnp.where(rows == lax.broadcasted_iota(jnp.int32, (N, N), 1), 1.0, 0.0).astype(jnp.float32)
+def halves(mine_ref, other_ref, side, core, index):
+    return jnp.where(core == index // side, mine_ref[index % side], other_ref[index % side])
+
+
+def factor_kernel(scale, edge_ref, mine_ref, other_ref, tri_ref, inv_ref, work):
+    for (i, j), index in GRAM.items():
+        work[i, :, j * N : (j + 1) * N] = halves(mine_ref, other_ref, GRAM_SIDE, edge_ref[2], index) * scale
+    zero = jnp.zeros((N, N), jnp.float32)
     for k in range(LAGS):
         for j in range(k):
-            tri_ref[k * N : (k + 1) * N, j * N : (j + 1) * N] = jnp.zeros((N, N), jnp.float32)
+            tri_ref[k * N : (k + 1) * N, j * N : (j + 1) * N] = zero
+            inv_ref[j * N : (j + 1) * N, k * N : (k + 1) * N] = zero
+            work[k, :, j * N : (j + 1) * N] = zero
 
     def finish(k, upper, inverse):
-        tri_ref[k * N : (k + 1) * N, k * N : (k + 1) * N] = upper
-        solved = exact(inverse, work[k, :, (k + 1) * N :], ((1,), (0,)))
-        work[k, :, (k + 1) * N :] = solved
-        if k < LAGS - 1:
-            tri_ref[k * N : (k + 1) * N, (k + 1) * N :] = solved[:, : (LAGS - 1 - k) * N]
+        lo, hi = k * N, (k + 1) * N
+        tri_ref[lo:hi, lo:hi] = upper
+        inv_ref[lo:hi, lo:hi] = inverse
+        columns = [work[k, :, j * N : (j + 1) * N] for j in range(LAGS) if j != k]
+        solved = stacked(inverse, jnp.concatenate(columns, 1), 1)
+        if k:
+            inv_ref[lo:hi, :lo] = solved[:, :lo]
+        if k == LAGS - 1:
+            return
+        tri_ref[lo:hi, hi:] = solved[:, lo:]
+        before = [solved[:, :lo]] if k else []
+        done = jnp.concatenate(before + [inverse, solved[:, lo:]], 1)
         for i in range(k + 1, LAGS):
-            lo = (i - k - 1) * N
-            work[i, :, i * N :] = work[i, :, i * N :] - exact(solved[:, lo : lo + N], solved[:, lo:], ((0,), (0,)))
+            across = jnp.concatenate([done[:, :hi], done[:, i * N :]], 1)
+            update = stacked(done[:, i * N : (i + 1) * N], across, 0)
+            work[i, :, :hi] -= update[:, :hi]
+            work[i, :, i * N :] -= update[:, hi:]
 
     def step(k, carry):
-        upper, inverse = factor(work[k, :, pl.ds(pl.multiple_of(k * N, N), N)], eye)
-        inv[k] = inverse
+        upper, inverse = factor(work[k, :, pl.ds(pl.multiple_of(k * N, N), N)])
         for which in range(LAGS):
             pl.when(k == which)(functools.partial(finish, which, upper, inverse))
         return carry
 
     lax.fori_loop(0, LAGS, step, 0)
-    for i in range(LAGS):
-        right[i * N : (i + 1) * N, :] = work[i, :, COLS:]
-    for j in range(LAGS):
-        lo, hi = j * N, (j + 1) * N
-        solved = exact(right[:, lo:hi], inv[j], ((1,), (1,)))
-        op_ref[:, lo:hi] = solved
-        if j < LAGS - 1:
-            right[:, hi:] = right[:, hi:] - exact(solved, tri_ref[lo:hi, hi:], ((1,), (0,)))
+
+
+def solve_kernel(scale, edge_ref, inv_ref, mine_ref, other_ref, op_ref, work):
+    for (i, j), index in CROSS.items():
+        block = halves(mine_ref, other_ref, CROSS_SIDE, edge_ref[2], index - len(GRAM))
+        work[i * N : (i + 1) * N, j * N : (j + 1) * N] = (block.T if i >= j else block) * scale
+    for lo in reversed(range(0, COLS, N)):
+        hi = lo + N
+        work[lo:hi, :] = exact(inv_ref[lo:hi, :hi], work[:hi, :], ((1,), (0,)))
+    for lo in range(0, COLS, N):
+        hi = lo + N
+        op_ref[:, lo:hi] = exact(work[:, :hi], inv_ref[lo:hi, :hi], ((1,), (1,)))
 
 
 def shifted(value, steps):
@@ -290,12 +343,12 @@
     return lax.all_to_all(value, AXES, 0, 0, axis_index_groups=groups)
 
 
-def fan(value, copies):
+def fan(value, copies, sizes):
     return pl.pallas_call(
         fan_kernel,
-        out_shape=jax.ShapeDtypeStruct((copies,) + value.shape[1:], jnp.float32),
+        out_shape=[jax.ShapeDtypeStruct((copies, size, N), jnp.float32) for size in sizes],
         in_specs=[pl.BlockSpec(memory_space=pltpu.VMEM)],
-        out_specs=pl.BlockSpec(memory_space=pltpu.VMEM),
+        out_specs=[pl.BlockSpec(memory_space=pltpu.VMEM)] * len(sizes),
         compiler_params=pltpu.CompilerParams(vmem_limit_bytes=VMEM_LIMIT),
         name="add_and_repeat",
     )(value)
@@ -322,25 +375,28 @@
         for x in range(CHIPS_X)
     ]
     plane = rows * CHIPS_X
-    half = keep + across_cores(give)
-    shares = trade(half.reshape(plane, SIDE * N // plane, N), planes)
-    shares = trade(fan(shares, depth), columns)
-    mine = trade(fan(shares, plane), planes).reshape(SIDE, N, N)
-    return mine, across_cores(mine)
+    shares = trade(keep + across_cores(give), planes)
+    (shares,) = fan(shares, depth, [shares.shape[1]])
+    few, many = GRAM_SIDE * N // plane, CROSS_SIDE * N // plane
+    gram, cross = fan(trade(shares, columns), plane, [few, many])
+    gram = trade(gram, planes)
+    gram, cross = lax.optimization_barrier((gram, cross))
+    gram = gram.reshape(GRAM_SIDE, N, N)
+    cross = trade(cross, planes).reshape(CROSS_SIDE, N, N)
+    return (gram, across_cores(gram)), cross
 
 
 def averaged_blocks(record, edge):
     count = record.shape[0]
     smem, vmem = pl.BlockSpec(memory_space=pltpu.SMEM), pl.BlockSpec(memory_space=pltpu.VMEM)
-    anywhere = pl.BlockSpec(memory_space=pl.ANY)
     params = pltpu.CompilerParams(vmem_limit_bytes=VMEM_LIMIT)
     head, rear = pl.pallas_call(
         carve_kernel,
         out_shape=[jax.ShapeDtypeStruct((SPAN + 8, N), jnp.float32), jax.ShapeDtypeStruct((SPAN, N), jnp.float32)],
-        in_specs=[anywhere],
+        in_specs=[pl.BlockSpec(memory_space=pltpu.HBM)],
         out_specs=[vmem, vmem],
         scratch_shapes=[pltpu.SemaphoreType.DMA((2,))],
-        compiler_params=params,
+        compiler_params=pltpu.CompilerParams(vmem_limit_bytes=62 * 2**20),
         name="carve",
     )(record)
     down, up = shifted(head, -1), shifted(rear, 1)
@@ -357,13 +413,15 @@
         cost_estimate=pl.CostEstimate(flops=4 * 10**9, bytes_accessed=8 * 2**20, transcendentals=0),
         name="local_products",
     )(edge, record)
-    side = jax.ShapeDtypeStruct((SIDE, N, N), jnp.float32)
+    members = lax.axis_size("grp") // 2 * CHIPS_X
+    side = jax.ShapeDtypeStruct((members, (GRAM_SIDE + CROSS_SIDE) * N // members, N), jnp.float32)
     keep, give = pl.pallas_call(
         halo_kernel,
         out_shape=[side, side],
         in_specs=[smem, vmem, vmem, vmem, vmem],
         out_specs=[vmem, vmem],
-        scratch_shapes=[pltpu.VMEM((SPAN, 4 * N), jnp.bfloat16)] * 2 + [pltpu.VMEM((2, SIDE, N, N), jnp.float32)],
+        scratch_shapes=[pltpu.VMEM((SPAN, 4 * N), jnp.bfloat16)] * 2
+        + [pltpu.VMEM((2, GRAM_SIDE * N, N), jnp.float32), pltpu.VMEM((2, CROSS_SIDE * N, N), jnp.float32)],
         compiler_params=params,
         cost_estimate=pl.CostEstimate(flops=3 * 10**9, bytes_accessed=9 * 2**20, transcendentals=0),
         name="halo_products",
@@ -376,24 +434,32 @@
     last_row = record.shape[0] * devices - (LAGS - 1) * DELAY - 1
     index = lax.axis_index(AXES)
     edge = jnp.stack([index == 0, index == devices - 1, lax.axis_index("grp") % 2]).astype(jnp.int32)
-    mine, other = averaged_blocks(record, edge)
+    gram, cross = averaged_blocks(record, edge)
     smem, vmem = pl.BlockSpec(memory_space=pltpu.SMEM), pl.BlockSpec(memory_space=pltpu.VMEM)
+    params = pltpu.CompilerParams(vmem_limit_bytes=VMEM_LIMIT)
     square = jax.ShapeDtypeStruct((COLS, COLS), jnp.float32)
-    return tuple(
-        pl.pallas_call(
-            functools.partial(tail_kernel, 1.0 / last_row),
-            out_shape=[square, square],
-            in_specs=[smem, vmem, vmem],
-            out_specs=[vmem, vmem],
-            scratch_shapes=[
-                pltpu.VMEM((LAGS, N, 2 * COLS), jnp.float32),
-                pltpu.VMEM((COLS, COLS), jnp.float32),
-                pltpu.VMEM((LAGS, N, N), jnp.float32),
-            ],
-            compiler_params=pltpu.CompilerParams(vmem_limit_bytes=VMEM_LIMIT),
-            name="factor_and_solve",
-        )(edge, mine, other)
-    )
+    triangle, inverse = pl.pallas_call(
+        functools.partial(factor_kernel, 1.0 / last_row),
+        out_shape=[square, square],
+        in_specs=[smem, vmem, vmem],
+        out_specs=[vmem, vmem],
+        scratch_shapes=[pltpu.VMEM((LAGS, N, COLS), jnp.float32)],
+        compiler_params=params,
+        cost_estimate=pl.CostEstimate(flops=20 * 10**9, bytes_accessed=4 * 2**20, transcendentals=0),
+        name="factor",
+    )(edge, *gram)
+    cross, triangle, inverse = lax.optimization_barrier((cross, triangle, inverse))
+    operator = pl.pallas_call(
+        functools.partial(solve_kernel, 1.0 / last_row),
+        out_shape=square,
+        in_specs=[smem] + [vmem] * 3,
+        out_specs=vmem,
+        scratch_shapes=[pltpu.VMEM((COLS, COLS), jnp.float32)],
+        compiler_params=params,
+        cost_estimate=pl.CostEstimate(flops=5 * 10**9, bytes_accessed=4 * 2**20, transcendentals=0),
+        name="solve",
+    )(edge, inverse, cross, across_cores(cross))
+    return triangle, operator
 
 
 def solution(mesh):

time: 131 us -> 129 us (0.985)
  blocking collectives: 50.7 us -> 46.2 us
  starting transfers between devices: 16.8 us -> 20.7 us
  waiting for transfers between devices: 21.4 us -> 19.6 us
    all_to_all x3, blocking collectives: 50.7 us -> 46.2 us  [trade(): return lax.all_to_all(value, AXES, 0, 0, axis_index_groups=groups)]
    all_to_all x0 -> x1, starting transfers between devices: none -> 3.75 us  [trade(): return lax.all_to_all(value, AXES, 0, 0, axis_index_groups=groups)]
    ppermute x2, waiting for transfers between devices: 17 us -> 15.3 us  [shifted(): lax.ppermute(value, AXES, [(source, source + steps) for source in range(l...]
    pallas_call x3 -> x4, Pallas kernels: 26 us -> 25.1 us  [the longest x1 18.9 us: on_device(): pl.pallas_call(functools.partial(factor_kernel, 1.0 / last_row), out_shap...]
    ppermute x2 -> x3, starting transfers between devices: 3.77 us -> 4 us  [across_cores(): lax.ppermute(value, 'grp', [(source, source ^ 1) for source in range(coun...]
    ppermute x2 -> x3, waiting for transfers between devices: 4.37 us -> 4.27 us  [across_cores(): lax.ppermute(value, 'grp', [(source, source ^ 1) for source in range(coun...]
  transfers between devices with their start and end apart: 4 -> 6, of which waited for: 3 -> 3; matrix products, arithmetic and copies ran while one was open for 0% -> 0% of each run, Pallas kernels for 5% -> 20%
where the time goes in v3:
time: 129 us; the launch traced here: 128 us
  blocking collectives  46.2 us (36%)
  Pallas kernels  39.1 us (30%)
  starting transfers between devices  20.7 us (16%)
  waiting for transfers between devices  19.6 us (15%)
  local copies, waits for them, and re-layouts  1.59 us (1%)
    all_to_all x3, blocking collectives, trade(): return lax.all_to_all(value, AXES, 0, 0, axis_index_groups=groups)  46.2 us
    pallas_call x1, Pallas kernels, on_device(): pl.pallas_call(functools.partial(factor_kernel, 1.0 / last_row), out_shap...  18.9 us
    ppermute x2, waiting for transfers between devices, shifted(): lax.ppermute(value, AXES, [(source, source + steps) for source in range(l...  15.3 us
    ppermute x2, starting transfers between devices, shifted(): lax.ppermute(value, AXES, [(source, source + steps) for source in range(l...  13 us
    pallas_call x1, Pallas kernels, averaged_blocks(): pl.pallas_call(local_kernel, out_shape=[jax.ShapeDtypeStruct((BLOCKS, N,...  6.31 us
    pallas_call x1, Pallas kernels, on_device(): pl.pallas_call(functools.partial(solve_kernel, 1.0 / last_row), out_shape...  5.32 us
    pallas_call x1, Pallas kernels, averaged_blocks(): pl.pallas_call(halo_kernel, out_shape=[side, side], in_specs=[smem, vmem,...  5.2 us
    ppermute x3, waiting for transfers between devices, across_cores(): lax.ppermute(value, 'grp', [(source, source ^ 1) for source in range(coun...  4.27 us
  transfers between devices with their start and end apart: 6, of which 3 were waited for; matrix products, arithmetic and copies ran while one was open for 0% of the time, Pallas kernels for 20%

profile of v3, /device:TPU:1, one launch (start us, length us, event | category | flops | bytes accessed | tf_op | source)
XLA Modules:
  0.0 128.1 jit_solution(2908651546026586802)
XLA Ops:
  0.6 2.5 %carve.1 = (f32[1544,128]{1,0:T(8,128)}, f32[1536,128]{1,0:T(8,128)}) custom-call(f32[4096,128]{1,0:T(8,128)} %rec_ref.3), custom_call_target="tpu_custom_call" | custom-call | tf_op jit(solution)/shard_map/carve/pallas_call | solution.py:393
  3.2 11.1 %collective-permute-start = (f32[1544,128]{1,0:T(8,128)}, f32[1544,128]{1,0:T(8,128)S(1)}, u32[]{:S(2)}, u32[]{:S(2)}) collective-permute-start(f32[1544,128]{1,0:T(8,128)} %get-tuple-element.19), channel_id=1, source_target_pairs={{1,0},{2,1},{3,2},{4,3},{5,4},{6,5},{7,6},{8,7},{9,8},{10,9},{11,1... | collective-permute-start | bytes 2371592 | tf_op jit(solution)/shard_map/ppermute | solution.py:337
  14.2 1.9 %collective-permute-start.1 = (f32[1536,128]{1,0:T(8,128)}, f32[1536,128]{1,0:T(8,128)S(1)}, u32[]{:S(2)}, u32[]{:S(2)}) collective-permute-start(f32[1536,128]{1,0:T(8,128)} %get-tuple-element.20), channel_id=1, source_target_pairs={{0,1},{1,2},{2,3},{3,4},{4,5},{5,6},{6,7},{7,8},{8,9},{9,10},{10,1... | collective-permute-start | bytes 2359304 | tf_op jit(solution)/shard_map/ppermute | solution.py:337
  16.2 0.1 pad_add_fusion.edge_ref
  16.3 0.0 copy-start
  16.3 1.6 %copy-done = f32[4096,128]{1,0:T(8,128)S(1)} copy-done((f32[4096,128]{1,0:T(8,128)S(1)}, f32[4096,128]{1,0:T(8,128)}, u32[]{:S(2)}) %copy-start) | copy-done | bytes 2097176
  17.9 6.3 %local_products.1 = (f32[26,128,128]{2,1,0:T(8,128)S(1)}, bf16[4096,512]{1,0:T(8,128)(2,1)}) custom-call(s32[3]{0:T(128)S(1)} %pad_add_fusion.edge_ref, f32[4096,128]{1,0:T(8,128)S(1)} %copy-done), custom_call_target="tpu_custom_call" | custom-call | flops 4000000000 | bytes 8388608 | tf_op jit(solution)/shard_map/local_products/pallas_call | solution.py:403
  24.2 15.3 %collective-permute-done.1.up_ref = f32[1536,128]{1,0:T(8,128)S(1)} collective-permute-done((f32[1536,128]{1,0:T(8,128)}, f32[1536,128]{1,0:T(8,128)S(1)}, u32[]{:S(2)}, u32[]{:S(2)}) %collective-permute-start.1) | collective-permute-done | bytes 786464 | tf_op jit(solution)/shard_map/ppermute | solution.py:337
  39.5 0.0 collective-permute-done.down_ref
  39.5 5.2 %halo_products.1 = (f32[16,104,128]{2,1,0:T(8,128)S(1)}, f32[16,104,128]{2,1,0:T(8,128)S(1)}) custom-call(s32[3]{0:T(128)S(1)} %pad_add_fusion.edge_ref, f32[26,128,128]{2,1,0:T(8,128)S(1)} %get-tuple-element.17.acc_ref, bf16[4096,512]{1,0:T(8,128)(2,1)} %get-tuple-element.18.split_ref, f32[1544,128]{1,0:T(8,128)S(1)} %collective-permute-done.down_ref, ...), custom_call_target="tpu_custom_call" | custom-call | flops 3000000000 | bytes 9437184 | tf_op jit(solution)/shard_map/halo_products/pallas_call | solution.py:418
  44.7 0.1 collective-permute-start.2
  44.8 2.4 %collective-permute-done.2 = f32[16,104,128]{2,1,0:T(8,128)S(1)} collective-permute-done((f32[16,104,128]{2,1,0:T(8,128)S(1)}, f32[16,104,128]{2,1,0:T(8,128)S(1)}, u32[]{:S(2)}, u32[]{:S(2)}) %collective-permute-start.2) | collective-permute-done | bytes 852000 | tf_op jit(solution)/shard_map/ppermute | solution.py:359
  47.1 0.1 add.12
  47.3 19.0 %all_to_all.20.in_ref = f32[16,104,128]{2,1,0:T(8,128)S(1)} all-to-all(f32[16,104,128]{2,1,0:T(8,128)S(1)} %add.12), channel_id=1, replica_groups={{0,1,2,3,64,65,66,67,128,129,130,131,192,193,194,195},{4,5,6,7,68,69,70..., dimensions={0} | all-to-all | bytes 1703936 | tf_op jit(solution)/shard_map/all_to_all | solution.py:343
  66.2 0.1 add_and_repeat.2
  66.3 16.1 %all_to_all.21.in_ref = f32[8,104,128]{2,1,0:T(8,128)S(1)} all-to-all(f32[8,104,128]{2,1,0:T(8,128)S(1)} %add_and_repeat.2), channel_id=1, replica_groups={{0,4,8,12,16,20,24,28},{1,5,9,13,17,21,25,29},{2,6,10,14,18,22,26,30},{..., dimensions={0} | all-to-all | bytes 851968 | tf_op jit(solution)/shard_map/all_to_all | solution.py:343
  82.4 0.9 add_and_repeat.3
  83.3 11.1 %all_to_all.22 = f32[16,40,128]{2,1,0:T(8,128)S(1)} all-to-all(f32[16,40,128]{2,1,0:T(8,128)S(1)} %get-tuple-element.23), channel_id=1, replica_groups={{0,1,2,3,64,65,66,67,128,129,130,131,192,193,194,195},{4,5,6,7,68,69,70..., dimensions={0} | all-to-all | bytes 655360 | tf_op jit(solution)/shard_map/all_to_all | solution.py:343
  94.4 3.9 %collective-permute-start.3 = (f32[5,128,128]{2,1,0:T(8,128)S(1)}, f32[5,128,128]{2,1,0:T(8,128)S(1)}, u32[]{:S(2)}, u32[]{:S(2)}) collective-permute-start(f32[5,128,128]{2,1,0:T(8,128)S(1)} %bitcast.7), channel_id=1, source_target_pairs={{0,32},{32,0},{64,96},{96,64},{128,160},{160,128},{192,224},{224,1... | collective-permute-start | bytes 983048 | tf_op jit(solution)/shard_map/ppermute | solution.py:359
  98.3 3.8 %all-to-all-start.3 = ((f32[16,64,128]{2,1,0:T(8,128)}), f32[16,64,128]{2,1,0:T(8,128)S(1)}, u32[]{:S(2)}, u32[]{:S(2)}) async-start(f32[16,64,128]{2,1,0:T(8,128)} %get-tuple-element.25), calls=%async_computation.3 | async-start | bytes 1048576 | tf_op jit(solution)/shard_map/all_to_all | solution.py:343
  102.0 0.0 collective-permute-done.3.other_ref
  102.0 18.9 %factor.1 = (f32[512,512]{1,0:T(8,128)}, f32[512,512]{1,0:T(8,128)S(1)}) custom-call(s32[3]{0:T(128)S(1)} %pad_add_fusion.edge_ref, f32[5,128,128]{2,1,0:T(8,128)S(1)} %bitcast.8, f32[5,128,128]{2,1,0:T(8,128)S(1)} %collective-permute-done.3.other_ref), custom_call_target="tpu_custom_call" | custom-call | flops 20000000000 | bytes 4194304 | tf_op jit(solution)/shard_map/factor/pallas_call | solution.py:441
  120.9 0.0 all-to-all-done.3
  120.9 0.0 collective-permute-start.4
  120.9 1.9 %collective-permute-done.4.other_ref = f32[8,128,128]{2,1,0:T(8,128)S(1)} collective-permute-done((f32[8,128,128]{2,1,0:T(8,128)S(1)}, f32[8,128,128]{2,1,0:T(8,128)S(1)}, u32[]{:S(2)}, u32[]{:S(2)}) %collective-permute-start.4) | collective-permute-done | bytes 524320 | tf_op jit(solution)/shard_map/ppermute | solution.py:359
  122.8 5.3 %solve.1 = f32[512,512]{1,0:T(8,128)} custom-call(s32[3]{0:T(128)S(1)} %pad_add_fusion.edge_ref, f32[512,512]{1,0:T(8,128)S(1)} %get-tuple-element.30.inv_ref, f32[8,128,128]{2,1,0:T(8,128)S(1)} %bitcast.6, f32[8,128,128]{2,1,0:T(8,128)S(1)} %collective-permute-done.4.other_ref), custom_call_target="tpu_custom_call" | custom-call | flops 5000000000 | bytes 4194304 | tf_op jit(solution)/shard_map/solve/pallas_call | solution.py:452
Async XLA Ops:
  3.2 36.3 %collective-permute-start = (f32[1544,128]{1,0:T(8,128)}, f32[1544,128]{1,0:T(8,128)S(1)}, u32[]{:S(2)}, u32[]{:S(2)}) collective-permute-start(f32[1544,128]{1,0:T(8,128)} %get-tuple-element.19), channel_id=1, source_target_pairs={{1,0},{2,1},{3,2},{4,3},{5,4},{6,5},{7,6},{8,7},{9,8},{10,9},{11,1... | collective-permute-start | bytes 2371592 | tf_op jit(solution)/shard_map/ppermute | solution.py:337
  14.2 25.2 %collective-permute-start.1 = (f32[1536,128]{1,0:T(8,128)}, f32[1536,128]{1,0:T(8,128)S(1)}, u32[]{:S(2)}, u32[]{:S(2)}) collective-permute-start(f32[1536,128]{1,0:T(8,128)} %get-tuple-element.20), channel_id=1, source_target_pairs={{0,1},{1,2},{2,3},{3,4},{4,5},{5,6},{6,7},{7,8},{8,9},{9,10},{10,1... | collective-permute-start | bytes 2359304 | tf_op jit(solution)/shard_map/ppermute | solution.py:337
  16.3 1.6 %copy-start = (f32[4096,128]{1,0:T(8,128)S(1)}, f32[4096,128]{1,0:T(8,128)}, u32[]{:S(2)}) copy-start(f32[4096,128]{1,0:T(8,128)} %rec_ref.3) | copy-start | bytes 6291460
  44.7 2.5 %collective-permute-start.2 = (f32[16,104,128]{2,1,0:T(8,128)S(1)}, f32[16,104,128]{2,1,0:T(8,128)S(1)}, u32[]{:S(2)}, u32[]{:S(2)}) collective-permute-start(f32[16,104,128]{2,1,0:T(8,128)S(1)} %get-tuple-element.22), channel_id=1, source_target_pairs={{0,32},{32,0},{64,96},{96,64},{128,160},{160,128},{192,224},{224,1... | collective-permute-start | bytes 2555912 | tf_op jit(solution)/shard_map/ppermute | solution.py:359
  94.4 7.7 %collective-permute-start.3 = (f32[5,128,128]{2,1,0:T(8,128)S(1)}, f32[5,128,128]{2,1,0:T(8,128)S(1)}, u32[]{:S(2)}, u32[]{:S(2)}) collective-permute-start(f32[5,128,128]{2,1,0:T(8,128)S(1)} %bitcast.7), channel_id=1, source_target_pairs={{0,32},{32,0},{64,96},{96,64},{128,160},{160,128},{192,224},{224,1... | collective-permute-start | bytes 983048 | tf_op jit(solution)/shard_map/ppermute | solution.py:359
  98.3 22.7 %all-to-all-start.3 = ((f32[16,64,128]{2,1,0:T(8,128)}), f32[16,64,128]{2,1,0:T(8,128)S(1)}, u32[]{:S(2)}, u32[]{:S(2)}) async-start(f32[16,64,128]{2,1,0:T(8,128)} %get-tuple-element.25), calls=%async_computation.3 | async-start | bytes 1048576 | tf_op jit(solution)/shard_map/all_to_all | solution.py:343
  120.9 1.9 %collective-permute-start.4 = (f32[8,128,128]{2,1,0:T(8,128)S(1)}, f32[8,128,128]{2,1,0:T(8,128)S(1)}, u32[]{:S(2)}, u32[]{:S(2)}) collective-permute-start(f32[8,128,128]{2,1,0:T(8,128)S(1)} %bitcast.5), channel_id=1, source_target_pairs={{0,32},{32,0},{64,96},{96,64},{128,160},{160,128},{192,224},{224,1... | collective-permute-start | bytes 1572872 | tf_op jit(solution)/shard_map/ppermute | solution.py:359

commit v4 on v3

--- a/solution.py
+++ b/solution.py
@@ -11,11 +11,11 @@
 DELAY = 1024
 N = 128
 COLS = LAGS * N
-HALF = DELAY // 2
-SPAN = DELAY + HALF
+CUT = 640
+DOWN, UP = DELAY + CUT, 2 * DELAY - CUT
 AXES = ("grp", "span")
 HIGHEST = lax.Precision.HIGHEST
-VMEM_LIMIT = 48 * 2**20
+VMEM_LIMIT = 24 * 2**20
 
 PAIRS = [(i, j) for i in range(LAGS) for j in range(i, LAGS)]
 GRAM = {pair: index for index, pair in enumerate(PAIRS)}
@@ -129,37 +129,33 @@
         copy.wait()
 
 
-def fan_kernel(in_ref, *out_refs):
+def fan_kernel(in_ref, out_ref):
     value = in_ref[0]
     for k in range(1, in_ref.shape[0]):
         value = value + in_ref[k]
-    start = 0
-    for out_ref in out_refs:
-        size = out_ref.shape[1]
-        for k in range(out_ref.shape[0]):
-            out_ref[k] = value[start : start + size]
-        start += size
+    for k in range(out_ref.shape[0]):
+        out_ref[k] = value
 
 
 def halo_kernel(edge_ref, acc_ref, split_ref, down_ref, up_ref, keep_ref, give_ref, below, above, gram, cross):
-    below[:, : 2 * N] = parts(down_ref[:SPAN, :])
-    below[:, 2 * N :] = parts(down_ref[1 : SPAN + 1, :])
+    below[:, : 2 * N] = parts(down_ref[:DOWN, :])
+    below[:, 2 * N :] = parts(down_ref[1 : DOWN + 1, :])
     above[:, : 2 * N] = parts(up_ref[...])
     own = split_ref[0:16, : 2 * N].astype(jnp.float32)[0:1]
     own = (own[:, :N] + own[:, N:]) * (1 - edge_ref[0]).astype(jnp.float32)
-    above[:, 2 * N :] = parts(jnp.concatenate([up_ref[1:SPAN, :], own], 0))
+    above[:, 2 * N :] = parts(jnp.concatenate([up_ref[1:UP, :], own], 0))
 
     def own_rows(start, size):
         return split_ref[start : start + size, :]
 
     pairs = {
         1: [(own_rows(3 * DELAY, DELAY), below[:DELAY, :])],
-        2: [(own_rows(2 * DELAY, DELAY), below[:DELAY, :]), (above[HALF:, :], own_rows(DELAY, DELAY))],
+        2: [(own_rows(2 * DELAY, DELAY), below[:DELAY, :]), (above[DELAY - CUT :, :], own_rows(DELAY, DELAY))],
         3: [
             (own_rows(DELAY, DELAY), below[:DELAY, :]),
-            (above[HALF:, :], own_rows(2 * DELAY, DELAY)),
-            (own_rows(2 * DELAY, HALF), below[DELAY:, :]),
-            (above[:HALF, :], own_rows(DELAY + HALF, HALF)),
+            (above[DELAY - CUT :, :], own_rows(2 * DELAY, DELAY)),
+            (own_rows(2 * DELAY, CUT), below[DELAY:, :]),
+            (above[: DELAY - CUT, :], own_rows(DELAY + CUT, DELAY - CUT)),
         ],
     }
     core = edge_ref[2]
@@ -218,12 +214,12 @@
     return high, mid, (rest - mid.astype(jnp.float32)).astype(jnp.bfloat16)
 
 
-def stacked(left, right, dim):
+def stacked(left, right, left_dim, right_dim):
     (a, b, c), (x, y, z) = three(left), three(right)
     return lax.dot_general(
-        jnp.concatenate([a, a, b, a, c, b], dim),
-        jnp.concatenate([x, y, x, z, x, y], 0),
-        (((dim,), (0,)), ((), ())),
+        jnp.concatenate([a, a, b, a, c, b], left_dim),
+        jnp.concatenate([x, y, x, z, x, y], right_dim),
+        (((left_dim,), (right_dim,)), ((), ())),
         preferred_element_type=jnp.float32,
     )
 
@@ -270,20 +266,29 @@
             upper = jnp.concatenate(uppers[-GROUP:], 0)
             columns = lax.broadcasted_iota(jnp.int32, upper.shape, 1)
             done = jnp.where(columns < 8 * end, jnp.concatenate(inverses[-GROUP:], 0), upper)
-            update = stacked(upper, done, 0)
+            update = stacked(upper, done, 0, 0)
             grouped = (lane >= 8 * (end - GROUP)) & (lane < 8 * end)
             for v in range(end, len(rows)):
                 rows[v] = jnp.where(grouped, 0.0, rows[v]) - update[8 * v : 8 * v + 8]
     return jnp.concatenate(uppers, 0), jnp.concatenate(inverses, 0)
 
 
-def halves(mine_ref, other_ref, side, core, index):
-    return jnp.where(core == index // side, mine_ref[index % side], other_ref[index % side])
-
-
-def factor_kernel(scale, edge_ref, mine_ref, other_ref, tri_ref, inv_ref, work):
+def tail_kernel(scale, edge_ref, mine_ref, other_ref, tri_ref, op_ref, gram, cross, work, inv, left):
+    core = edge_ref[2]
+    few = gram.shape[1] // mine_ref.shape[0]
+    many = cross.shape[1] // mine_ref.shape[0]
+    for side, ref in ((core, mine_ref), (1 - core, other_ref)):
+        for m in range(ref.shape[0]):
+            gram[side, m * few : (m + 1) * few] = ref[m, :few] * scale
+            cross[side, m * many : (m + 1) * many] = ref[m, few:] * scale
+    factor_rows(gram, tri_ref, inv, work)
+    solve_rows(cross, inv, op_ref, left)
+
+
+def factor_rows(gram, tri_ref, inv_ref, work):
     for (i, j), index in GRAM.items():
-        work[i, :, j * N : (j + 1) * N] = halves(mine_ref, other_ref, GRAM_SIDE, edge_ref[2], index) * scale
+        row = index % GRAM_SIDE * N
+        work[i, :, j * N : (j + 1) * N] = gram[index // GRAM_SIDE, row : row + N]
     zero = jnp.zeros((N, N), jnp.float32)
     for k in range(LAGS):
         for j in range(k):
@@ -296,7 +301,7 @@
         tri_ref[lo:hi, lo:hi] = upper
         inv_ref[lo:hi, lo:hi] = inverse
         columns = [work[k, :, j * N : (j + 1) * N] for j in range(LAGS) if j != k]
-        solved = stacked(inverse, jnp.concatenate(columns, 1), 1)
+        solved = stacked(inverse, jnp.concatenate(columns, 1), 1, 0)
         if k:
             inv_ref[lo:hi, :lo] = solved[:, :lo]
         if k == LAGS - 1:
@@ -306,7 +311,7 @@
         done = jnp.concatenate(before + [inverse, solved[:, lo:]], 1)
         for i in range(k + 1, LAGS):
             across = jnp.concatenate([done[:, :hi], done[:, i * N :]], 1)
-            update = stacked(done[:, i * N : (i + 1) * N], across, 0)
+            update = stacked(done[:, i * N : (i + 1) * N], across, 0, 0)
             work[i, :, :hi] -= update[:, :hi]
             work[i, :, i * N :] -= update[:, hi:]
 
@@ -319,16 +324,18 @@
     lax.fori_loop(0, LAGS, step, 0)
 
 
-def solve_kernel(scale, edge_ref, inv_ref, mine_ref, other_ref, op_ref, work):
+def solve_rows(cross, inv_ref, op_ref, work):
     for (i, j), index in CROSS.items():
-        block = halves(mine_ref, other_ref, CROSS_SIDE, edge_ref[2], index - len(GRAM))
-        work[i * N : (i + 1) * N, j * N : (j + 1) * N] = (block.T if i >= j else block) * scale
+        index -= len(GRAM)
+        row = index % CROSS_SIDE * N
+        block = cross[index // CROSS_SIDE, row : row + N]
+        work[i * N : (i + 1) * N, j * N : (j + 1) * N] = block.T if i >= j else block
     for lo in reversed(range(0, COLS, N)):
         hi = lo + N
-        work[lo:hi, :] = exact(inv_ref[lo:hi, :hi], work[:hi, :], ((1,), (0,)))
+        work[lo:hi, :] = stacked(inv_ref[lo:hi, :hi], work[:hi, :], 1, 0)
     for lo in range(0, COLS, N):
         hi = lo + N
-        op_ref[:, lo:hi] = exact(work[:, :hi], inv_ref[lo:hi, :hi], ((1,), (1,)))
+        op_ref[:, lo:hi] = stacked(work[:, :hi], inv_ref[lo:hi, :hi], 1, 1)
 
 
 def shifted(value, steps):
@@ -343,12 +350,12 @@
     return lax.all_to_all(value, AXES, 0, 0, axis_index_groups=groups)
 
 
-def fan(value, copies, sizes):
+def fan(value, copies):
     return pl.pallas_call(
         fan_kernel,
-        out_shape=[jax.ShapeDtypeStruct((copies, size, N), jnp.float32) for size in sizes],
+        out_shape=jax.ShapeDtypeStruct((copies,) + value.shape[1:], jnp.float32),
         in_specs=[pl.BlockSpec(memory_space=pltpu.VMEM)],
-        out_specs=[pl.BlockSpec(memory_space=pltpu.VMEM)] * len(sizes),
+        out_specs=pl.BlockSpec(memory_space=pltpu.VMEM),
         compiler_params=pltpu.CompilerParams(vmem_limit_bytes=VMEM_LIMIT),
         name="add_and_repeat",
     )(value)
@@ -376,14 +383,9 @@
     ]
     plane = rows * CHIPS_X
     shares = trade(keep + across_cores(give), planes)
-    (shares,) = fan(shares, depth, [shares.shape[1]])
-    few, many = GRAM_SIDE * N // plane, CROSS_SIDE * N // plane
-    gram, cross = fan(trade(shares, columns), plane, [few, many])
-    gram = trade(gram, planes)
-    gram, cross = lax.optimization_barrier((gram, cross))
-    gram = gram.reshape(GRAM_SIDE, N, N)
-    cross = trade(cross, planes).reshape(CROSS_SIDE, N, N)
-    return (gram, across_cores(gram)), cross
+    shares = fan(shares, depth)
+    mine = trade(fan(trade(shares, columns), plane), planes)
+    return mine, across_cores(mine)
 
 
 def averaged_blocks(record, edge):
@@ -392,7 +394,7 @@
     params = pltpu.CompilerParams(vmem_limit_bytes=VMEM_LIMIT)
     head, rear = pl.pallas_call(
         carve_kernel,
-        out_shape=[jax.ShapeDtypeStruct((SPAN + 8, N), jnp.float32), jax.ShapeDtypeStruct((SPAN, N), jnp.float32)],
+        out_shape=[jax.ShapeDtypeStruct((DOWN + 8, N), jnp.float32), jax.ShapeDtypeStruct((UP, N), jnp.float32)],
         in_specs=[pl.BlockSpec(memory_space=pltpu.HBM)],
         out_specs=[vmem, vmem],
         scratch_shapes=[pltpu.SemaphoreType.DMA((2,))],
@@ -420,7 +422,7 @@
         out_shape=[side, side],
         in_specs=[smem, vmem, vmem, vmem, vmem],
         out_specs=[vmem, vmem],
-        scratch_shapes=[pltpu.VMEM((SPAN, 4 * N), jnp.bfloat16)] * 2
+        scratch_shapes=[pltpu.VMEM((DOWN, 4 * N), jnp.bfloat16), pltpu.VMEM((UP, 4 * N), jnp.bfloat16)]
         + [pltpu.VMEM((2, GRAM_SIDE * N, N), jnp.float32), pltpu.VMEM((2, CROSS_SIDE * N, N), jnp.float32)],
         compiler_params=params,
         cost_estimate=pl.CostEstimate(flops=3 * 10**9, bytes_accessed=9 * 2**20, transcendentals=0),
@@ -434,32 +436,26 @@
     last_row = record.shape[0] * devices - (LAGS - 1) * DELAY - 1
     index = lax.axis_index(AXES)
     edge = jnp.stack([index == 0, index == devices - 1, lax.axis_index("grp") % 2]).astype(jnp.int32)
-    gram, cross = averaged_blocks(record, edge)
+    mine, other = averaged_blocks(record, edge)
     smem, vmem = pl.BlockSpec(memory_space=pltpu.SMEM), pl.BlockSpec(memory_space=pltpu.VMEM)
-    params = pltpu.CompilerParams(vmem_limit_bytes=VMEM_LIMIT)
     square = jax.ShapeDtypeStruct((COLS, COLS), jnp.float32)
-    triangle, inverse = pl.pallas_call(
-        functools.partial(factor_kernel, 1.0 / last_row),
-        out_shape=[square, square],
-        in_specs=[smem, vmem, vmem],
-        out_specs=[vmem, vmem],
-        scratch_shapes=[pltpu.VMEM((LAGS, N, COLS), jnp.float32)],
-        compiler_params=params,
-        cost_estimate=pl.CostEstimate(flops=20 * 10**9, bytes_accessed=4 * 2**20, transcendentals=0),
-        name="factor",
-    )(edge, *gram)
-    cross, triangle, inverse = lax.optimization_barrier((cross, triangle, inverse))
-    operator = pl.pallas_call(
-        functools.partial(solve_kernel, 1.0 / last_row),
-        out_shape=square,
-        in_specs=[smem] + [vmem] * 3,
-        out_specs=vmem,
-        scratch_shapes=[pltpu.VMEM((COLS, COLS), jnp.float32)],
-        compiler_params=params,
-        cost_estimate=pl.CostEstimate(flops=5 * 10**9, bytes_accessed=4 * 2**20, transcendentals=0),
-        name="solve",
-    )(edge, inverse, cross, across_cores(cross))
-    return triangle, operator
+    return tuple(
+        pl.pallas_call(
+            functools.partial(tail_kernel, 1.0 / last_row),
+            out_shape=[square, square],
+            in_specs=[smem, vmem, vmem],
+            out_specs=[vmem, vmem],
+            scratch_shapes=[
+                pltpu.VMEM((2, GRAM_SIDE * N, N), jnp.float32),
+                pltpu.VMEM((2, CROSS_SIDE * N, N), jnp.float32),
+                pltpu.VMEM((LAGS, N, COLS), jnp.float32),
+                pltpu.VMEM((COLS, COLS), jnp.float32),
+                pltpu.VMEM((COLS, COLS), jnp.float32),
+            ],
+            compiler_params=pltpu.CompilerParams(vmem_limit_bytes=VMEM_LIMIT),
+            name="factor_and_solve",
+        )(edge, mine, other)
+    )
 
 
 def solution(mesh):

time: 129 us -> 124 us (0.961)
  Pallas kernels: 39.1 us -> 33.2 us
  blocking collectives: 46.2 us -> 50.7 us
  starting transfers between devices: 20.7 us -> 16.8 us
    all_to_all x3, blocking collectives: 46.2 us -> 50.7 us  [trade(): return lax.all_to_all(value, AXES, 0, 0, axis_index_groups=groups)]
    all_to_all x1 -> x0, starting transfers between devices: 3.75 us -> none  [trade(): return lax.all_to_all(value, AXES, 0, 0, axis_index_groups=groups)]
    pallas_call x5 -> x4, Pallas kernels: 27.6 us -> 25.1 us  [the longest x1 22.4 us: on_device(): pl.pallas_call(functools.partial(tail_kernel, 1.0 / last_row), out_shape=...]
    pallas_call x1, Pallas kernels: 6.31 us -> 4.44 us  [averaged_blocks(): pl.pallas_call(local_kernel, out_shape=[jax.ShapeDtypeStruct((BLOCKS, N,...]
    pallas_call x1, Pallas kernels: 5.2 us -> 3.71 us  [averaged_blocks(): pl.pallas_call(halo_kernel, out_shape=[side, side], in_specs=[smem, vmem,...]
    ppermute x3 -> x2, starting transfers between devices: 4 us -> 3.77 us  [across_cores(): lax.ppermute(value, 'grp', [(source, source ^ 1) for source in range(coun...]
    ppermute x3 -> x2, waiting for transfers between devices: 4.27 us -> 4.37 us  [across_cores(): lax.ppermute(value, 'grp', [(source, source ^ 1) for source in range(coun...]
  transfers between devices with their start and end apart: 6 -> 4, of which waited for: 3 -> 3; matrix products, arithmetic and copies ran while one was open for 0% -> 0% of each run, Pallas kernels for 20% -> 4%
where the time goes in v4:
time: 124 us; the launch traced here: 123 us
  blocking collectives  50.7 us (41%)
  Pallas kernels  33.2 us (27%)
  waiting for transfers between devices  20.1 us (16%)
  starting transfers between devices  16.8 us (14%)
  local copies, waits for them, and re-layouts  1.59 us (1%)
    all_to_all x3, blocking collectives, trade(): return lax.all_to_all(value, AXES, 0, 0, axis_index_groups=groups)  50.7 us
    pallas_call x1, Pallas kernels, on_device(): pl.pallas_call(functools.partial(tail_kernel, 1.0 / last_row), out_shape=...  22.4 us
    ppermute x2, waiting for transfers between devices, shifted(): lax.ppermute(value, AXES, [(source, source + steps) for source in range(l...  15.8 us
    ppermute x2, starting transfers between devices, shifted(): lax.ppermute(value, AXES, [(source, source + steps) for source in range(l...  13 us
    pallas_call x1, Pallas kernels, averaged_blocks(): pl.pallas_call(local_kernel, out_shape=[jax.ShapeDtypeStruct((BLOCKS, N,...  4.44 us
    ppermute x2, waiting for transfers between devices, across_cores(): lax.ppermute(value, 'grp', [(source, source ^ 1) for source in range(coun...  4.37 us
    ppermute x2, starting transfers between devices, across_cores(): lax.ppermute(value, 'grp', [(source, source ^ 1) for source in range(coun...  3.77 us
    pallas_call x1, Pallas kernels, averaged_blocks(): pl.pallas_call(halo_kernel, out_shape=[side, side], in_specs=[smem, vmem,...  3.71 us
  transfers between devices with their start and end apart: 4, of which 3 were waited for; matrix products, arithmetic and copies ran while one was open for 0% of the time, Pallas kernels for 4%

profile of v4, /device:TPU:1, one launch (start us, length us, event | category | flops | bytes accessed | tf_op | source)
XLA Modules:
  0.0 123.3 jit_solution(1381695801115501679)
XLA Ops:
  0.6 2.5 %carve.1 = (f32[1672,128]{1,0:T(8,128)}, f32[1408,128]{1,0:T(8,128)}) custom-call(f32[4096,128]{1,0:T(8,128)} %rec_ref.3), custom_call_target="tpu_custom_call" | custom-call | tf_op jit(solution)/shard_map/carve/pallas_call | solution.py:395
  3.2 11.1 %collective-permute-start = (f32[1672,128]{1,0:T(8,128)}, f32[1672,128]{1,0:T(8,128)S(1)}, u32[]{:S(2)}, u32[]{:S(2)}) collective-permute-start(f32[1672,128]{1,0:T(8,128)} %get-tuple-element.10), channel_id=1, source_target_pairs={{1,0},{2,1},{3,2},{4,3},{5,4},{6,5},{7,6},{8,7},{9,8},{10,9},{11,1... | collective-permute-start | bytes 2568200 | tf_op jit(solution)/shard_map/ppermute | solution.py:344
  14.2 1.9 %collective-permute-start.1 = (f32[1408,128]{1,0:T(8,128)}, f32[1408,128]{1,0:T(8,128)S(1)}, u32[]{:S(2)}, u32[]{:S(2)}) collective-permute-start(f32[1408,128]{1,0:T(8,128)} %get-tuple-element.11), channel_id=1, source_target_pairs={{0,1},{1,2},{2,3},{3,4},{4,5},{5,6},{6,7},{7,8},{8,9},{9,10},{10,1... | collective-permute-start | bytes 2162696 | tf_op jit(solution)/shard_map/ppermute | solution.py:344
  16.2 0.1 pad_add_fusion.edge_ref
  16.3 0.0 copy-start
  16.3 1.6 %copy-done = f32[4096,128]{1,0:T(8,128)S(1)} copy-done((f32[4096,128]{1,0:T(8,128)S(1)}, f32[4096,128]{1,0:T(8,128)}, u32[]{:S(2)}) %copy-start) | copy-done | bytes 2097176
  17.9 4.4 %local_products.1 = (f32[26,128,128]{2,1,0:T(8,128)S(1)}, bf16[4096,512]{1,0:T(8,128)(2,1)S(1)}) custom-call(s32[3]{0:T(128)S(1)} %pad_add_fusion.edge_ref, f32[4096,128]{1,0:T(8,128)S(1)} %copy-done), custom_call_target="tpu_custom_call" | custom-call | flops 4000000000 | bytes 8388608 | tf_op jit(solution)/shard_map/local_products/pallas_call | solution.py:405
  22.3 15.8 %collective-permute-done.1.up_ref = f32[1408,128]{1,0:T(8,128)S(1)} collective-permute-done((f32[1408,128]{1,0:T(8,128)}, f32[1408,128]{1,0:T(8,128)S(1)}, u32[]{:S(2)}, u32[]{:S(2)}) %collective-permute-start.1) | collective-permute-done | bytes 720928 | tf_op jit(solution)/shard_map/ppermute | solution.py:344
  38.1 0.0 collective-permute-done.down_ref
  38.1 3.7 %halo_products.1 = (f32[16,104,128]{2,1,0:T(8,128)S(1)}, f32[16,104,128]{2,1,0:T(8,128)S(1)}) custom-call(s32[3]{0:T(128)S(1)} %pad_add_fusion.edge_ref, f32[26,128,128]{2,1,0:T(8,128)S(1)} %get-tuple-element.8.acc_ref, bf16[4096,512]{1,0:T(8,128)(2,1)S(1)} %get-tuple-element.9.split_ref, f32[1672,128]{1,0:T(8,128)S(1)} %collective-permute-done.down_ref, ...), custom_call_target="tpu_custom_call" | custom-call | flops 3000000000 | bytes 9437184 | tf_op jit(solution)/shard_map/halo_products/pallas_call | solution.py:420
  41.8 0.1 collective-permute-start.2
  41.9 2.4 %collective-permute-done.2 = f32[16,104,128]{2,1,0:T(8,128)S(1)} collective-permute-done((f32[16,104,128]{2,1,0:T(8,128)S(1)}, f32[16,104,128]{2,1,0:T(8,128)S(1)}, u32[]{:S(2)}, u32[]{:S(2)}) %collective-permute-start.2) | collective-permute-done | bytes 852000 | tf_op jit(solution)/shard_map/ppermute | solution.py:366
  44.2 0.1 add.12
  44.4 19.0 %all_to_all.15.in_ref = f32[16,104,128]{2,1,0:T(8,128)S(1)} all-to-all(f32[16,104,128]{2,1,0:T(8,128)S(1)} %add.12), channel_id=1, replica_groups={{0,1,2,3,64,65,66,67,128,129,130,131,192,193,194,195},{4,5,6,7,68,69,70..., dimensions={0} | all-to-all | bytes 1703936 | tf_op jit(solution)/shard_map/all_to_all | solution.py:350
  63.3 0.1 add_and_repeat.2
  63.4 16.1 %all_to_all.16.in_ref = f32[8,104,128]{2,1,0:T(8,128)S(1)} all-to-all(f32[8,104,128]{2,1,0:T(8,128)S(1)} %add_and_repeat.2), channel_id=1, replica_groups={{0,4,8,12,16,20,24,28},{1,5,9,13,17,21,25,29},{2,6,10,14,18,22,26,30},{..., dimensions={0} | all-to-all | bytes 851968 | tf_op jit(solution)/shard_map/all_to_all | solution.py:350
  79.5 0.1 add_and_repeat.3
  79.6 15.6 %all_to_all.17.mine_ref = f32[16,104,128]{2,1,0:T(8,128)S(1)} all-to-all(f32[16,104,128]{2,1,0:T(8,128)S(1)} %add_and_repeat.3), channel_id=1, replica_groups={{0,1,2,3,64,65,66,67,128,129,130,131,192,193,194,195},{4,5,6,7,68,69,70..., dimensions={0} | all-to-all | bytes 1703936 | tf_op jit(solution)/shard_map/all_to_all | solution.py:350
  95.2 3.7 %collective-permute-start.3 = (f32[16,104,128]{2,1,0:T(8,128)S(1)}, f32[16,104,128]{2,1,0:T(8,128)S(1)}, u32[]{:S(2)}, u32[]{:S(2)}) collective-permute-start(f32[16,104,128]{2,1,0:T(8,128)S(1)} %all_to_all.17.mine_ref), channel_id=1, source_target_pairs={{0,32},{32,0},{64,96},{96,64},{128,160},{160,128},{192,224},{224,1... | collective-permute-start | bytes 2555912 | tf_op jit(solution)/shard_map/ppermute | solution.py:366
  98.9 2.0 %collective-permute-done.3.other_ref = f32[16,104,128]{2,1,0:T(8,128)S(1)} collective-permute-done((f32[16,104,128]{2,1,0:T(8,128)S(1)}, f32[16,104,128]{2,1,0:T(8,128)S(1)}, u32[]{:S(2)}, u32[]{:S(2)}) %collective-permute-start.3) | collective-permute-done | bytes 852000 | tf_op jit(solution)/shard_map/ppermute | solution.py:366
  100.9 22.4 %factor_and_solve.1 = (f32[512,512]{1,0:T(8,128)}, f32[512,512]{1,0:T(8,128)}) custom-call(s32[3]{0:T(128)S(1)} %pad_add_fusion.edge_ref, f32[16,104,128]{2,1,0:T(8,128)S(1)} %all_to_all.17.mine_ref, f32[16,104,128]{2,1,0:T(8,128)S(1)} %collective-permute-done.3.other_ref), custom_call_target="tpu_custom_call" | custom-call | tf_op jit(solution)/shard_map/factor_and_solve/pallas_call | solution.py:443
Async XLA Ops:
  3.2 34.9 %collective-permute-start = (f32[1672,128]{1,0:T(8,128)}, f32[1672,128]{1,0:T(8,128)S(1)}, u32[]{:S(2)}, u32[]{:S(2)}) collective-permute-start(f32[1672,128]{1,0:T(8,128)} %get-tuple-element.10), channel_id=1, source_target_pairs={{1,0},{2,1},{3,2},{4,3},{5,4},{6,5},{7,6},{8,7},{9,8},{10,9},{11,1... | collective-permute-start | bytes 2568200 | tf_op jit(solution)/shard_map/ppermute | solution.py:344
  14.2 23.8 %collective-permute-start.1 = (f32[1408,128]{1,0:T(8,128)}, f32[1408,128]{1,0:T(8,128)S(1)}, u32[]{:S(2)}, u32[]{:S(2)}) collective-permute-start(f32[1408,128]{1,0:T(8,128)} %get-tuple-element.11), channel_id=1, source_target_pairs={{0,1},{1,2},{2,3},{3,4},{4,5},{5,6},{6,7},{7,8},{8,9},{9,10},{10,1... | collective-permute-start | bytes 2162696 | tf_op jit(solution)/shard_map/ppermute | solution.py:344
  16.3 1.6 %copy-start = (f32[4096,128]{1,0:T(8,128)S(1)}, f32[4096,128]{1,0:T(8,128)}, u32[]{:S(2)}) copy-start(f32[4096,128]{1,0:T(8,128)} %rec_ref.3) | copy-start | bytes 6291460
  41.8 2.5 %collective-permute-start.2 = (f32[16,104,128]{2,1,0:T(8,128)S(1)}, f32[16,104,128]{2,1,0:T(8,128)S(1)}, u32[]{:S(2)}, u32[]{:S(2)}) collective-permute-start(f32[16,104,128]{2,1,0:T(8,128)S(1)} %get-tuple-element.13), channel_id=1, source_target_pairs={{0,32},{32,0},{64,96},{96,64},{128,160},{160,128},{192,224},{224,1... | collective-permute-start | bytes 2555912 | tf_op jit(solution)/shard_map/ppermute | solution.py:366
  95.2 5.7 %collective-permute-start.3 = (f32[16,104,128]{2,1,0:T(8,128)S(1)}, f32[16,104,128]{2,1,0:T(8,128)S(1)}, u32[]{:S(2)}, u32[]{:S(2)}) collective-permute-start(f32[16,104,128]{2,1,0:T(8,128)S(1)} %all_to_all.17.mine_ref), channel_id=1, source_target_pairs={{0,32},{32,0},{64,96},{96,64},{128,160},{160,128},{192,224},{224,1... | collective-permute-start | bytes 2555912 | tf_op jit(solution)/shard_map/ppermute | solution.py:366

commit v5 on v4

--- a/solution.py
+++ b/solution.py
@@ -23,6 +23,7 @@
 BLOCKS = len(GRAM) + len(CROSS)
 GRAM_SIDE, CROSS_SIDE = len(GRAM) // 2, len(CROSS) // 2
 CHIPS_X = 4
+CARVE = 2
 GROUP = 4
 
 
@@ -117,15 +118,24 @@
                 out_ref[CROSS[i, j]] -= exact(c, a, outer) if i >= j else exact(a, c, outer)
 
 
-def carve_kernel(rec_ref, head_ref, rear_ref, sems):
-    head, rear = head_ref.shape[0], rear_ref.shape[0]
-    copies = [
-        pltpu.make_async_copy(rec_ref.at[:head], head_ref, sems.at[0]),
-        pltpu.make_async_copy(rec_ref.at[rec_ref.shape[0] - rear :], rear_ref, sems.at[1]),
-    ]
-    for copy in copies:
+def carve_kernel(rec_ref, head_ref, rear_ref, held, in_sems, out_sems):
+    count, parts_of = rec_ref.shape[0], CARVE
+    pieces = []
+    for ref, start in ((head_ref, 0), (rear_ref, count - rear_ref.shape[0])):
+        size = ref.shape[0] // parts_of
+        pieces += [(ref, start, p * size, size) for p in range(parts_of)]
+    arrivals, departures, place = [], [], 0
+    for n, (ref, start, offset, size) in enumerate(pieces):
+        slot = held.at[place : place + size]
+        arrivals.append(pltpu.make_async_copy(rec_ref.at[start + offset : start + offset + size], slot, in_sems.at[n]))
+        departures.append(pltpu.make_async_copy(slot, ref.at[offset : offset + size], out_sems.at[n]))
+        place += size
+    for copy in arrivals:
         copy.start()
-    for copy in copies:
+    for arrival, departure in zip(arrivals, departures):
+        arrival.wait()
+        departure.start()
+    for copy in departures:
         copy.wait()
 
 
@@ -224,7 +234,7 @@
     )
 
 
-def factor(matrix):
+def factor(matrix, between):
     sub = lax.broadcasted_iota(jnp.int32, (8, N), 0)
     lane = lax.broadcasted_iota(jnp.int32, (8, N), 1)
     rows = [matrix[r : r + 8] for r in range(0, N, 8)]
@@ -261,6 +271,7 @@
         root = lax.rsqrt(pivots)
         uppers.append(jnp.where(lane >= sub + first, top * root, 0.0))
         inverses.append(grown * root)
+        between()
         end = k + 1
         if end % GROUP == 0 and end < len(rows):
             upper = jnp.concatenate(uppers[-GROUP:], 0)
@@ -281,61 +292,79 @@
         for m in range(ref.shape[0]):
             gram[side, m * few : (m + 1) * few] = ref[m, :few] * scale
             cross[side, m * many : (m + 1) * many] = ref[m, few:] * scale
-    factor_rows(gram, tri_ref, inv, work)
-    solve_rows(cross, inv, op_ref, left)
-
-
-def factor_rows(gram, tri_ref, inv_ref, work):
-    for (i, j), index in GRAM.items():
-        row = index % GRAM_SIDE * N
-        work[i, :, j * N : (j + 1) * N] = gram[index // GRAM_SIDE, row : row + N]
+    factor_and_solve(gram, cross, tri_ref, op_ref, inv, work, left)
+
+
+def factor_and_solve(gram, cross, tri_ref, op_ref, inv_ref, work, left):
+    def block(k):
+        return slice(k * N, (k + 1) * N)
+
     zero = jnp.zeros((N, N), jnp.float32)
     for k in range(LAGS):
         for j in range(k):
-            tri_ref[k * N : (k + 1) * N, j * N : (j + 1) * N] = zero
-            inv_ref[j * N : (j + 1) * N, k * N : (k + 1) * N] = zero
-            work[k, :, j * N : (j + 1) * N] = zero
-
-    def finish(k, upper, inverse):
-        lo, hi = k * N, (k + 1) * N
-        tri_ref[lo:hi, lo:hi] = upper
-        inv_ref[lo:hi, lo:hi] = inverse
-        columns = [work[k, :, j * N : (j + 1) * N] for j in range(LAGS) if j != k]
-        solved = stacked(inverse, jnp.concatenate(columns, 1), 1, 0)
+            tri_ref[block(k), block(j)] = zero
+            inv_ref[block(j), block(k)] = zero
+            work[block(k), block(j)] = zero
+    for (i, j), index in GRAM.items():
+        row = index % GRAM_SIDE * N
+        work[block(i), block(j)] = gram[index // GRAM_SIDE, row : row + N]
+    waiting = []
+
+    def between():
+        if waiting:
+            waiting.pop(0)()
+
+    def fetch(i, j):
+        index = CROSS[i, j] - len(GRAM)
+        row = index % CROSS_SIDE * N
+        value = cross[index // CROSS_SIDE, row : row + N]
+        left[block(i), block(j)] = value.T if i >= j else value
+
+    def solve_side(k, inverse, target, source, columns):
+        target[block(k), columns] = stacked(inverse, source[block(k), columns], 1, 0)
+
+    def update(k, i, target, source, columns):
+        target[block(i), columns] -= stacked(tri_ref[block(k), block(i)], source[block(k), columns], 0, 0)
+
+    def project(rows, j):
+        known = slice(0, (j + 1) * N)
+        op_ref[rows, block(j)] = stacked(left[rows, known], inv_ref[block(j), known], 1, 1)
+
+    def later(function, *args):
+        waiting.append(functools.partial(function, *args))
+
+    for i in range(LAGS):
+        for j in range(LAGS):
+            later(fetch, i, j)
+    everything = slice(0, COLS)
+    for k in range(LAGS):
+        upper, inverse = factor(work[block(k), block(k)], between)
+        while waiting:
+            between()
+        tri_ref[block(k), block(k)] = upper
+        inv_ref[block(k), block(k)] = inverse
+        if k + 1 < LAGS:
+            solve_side(k, inverse, tri_ref, work, block(k + 1))
+            update(k, k + 1, work, tri_ref, block(k + 1))
+        if k + 2 < LAGS:
+            later(solve_side, k, inverse, tri_ref, work, slice((k + 2) * N, COLS))
         if k:
-            inv_ref[lo:hi, :lo] = solved[:, :lo]
-        if k == LAGS - 1:
-            return
-        tri_ref[lo:hi, hi:] = solved[:, lo:]
-        before = [solved[:, :lo]] if k else []
-        done = jnp.concatenate(before + [inverse, solved[:, lo:]], 1)
+            later(solve_side, k, inverse, inv_ref, work, slice(0, k * N))
+        later(solve_side, k, inverse, left, left, everything)
         for i in range(k + 1, LAGS):
-            across = jnp.concatenate([done[:, :hi], done[:, i * N :]], 1)
-            update = stacked(done[:, i * N : (i + 1) * N], across, 0, 0)
-            work[i, :, :hi] -= update[:, :hi]
-            work[i, :, i * N :] -= update[:, hi:]
-
-    def step(k, carry):
-        upper, inverse = factor(work[k, :, pl.ds(pl.multiple_of(k * N, N), N)])
-        for which in range(LAGS):
-            pl.when(k == which)(functools.partial(finish, which, upper, inverse))
-        return carry
-
-    lax.fori_loop(0, LAGS, step, 0)
-
-
-def solve_rows(cross, inv_ref, op_ref, work):
-    for (i, j), index in CROSS.items():
-        index -= len(GRAM)
-        row = index % CROSS_SIDE * N
-        block = cross[index // CROSS_SIDE, row : row + N]
-        work[i * N : (i + 1) * N, j * N : (j + 1) * N] = block.T if i >= j else block
-    for lo in reversed(range(0, COLS, N)):
-        hi = lo + N
-        work[lo:hi, :] = stacked(inv_ref[lo:hi, :hi], work[:hi, :], 1, 0)
-    for lo in range(0, COLS, N):
-        hi = lo + N
-        op_ref[:, lo:hi] = stacked(work[:, :hi], inv_ref[lo:hi, :hi], 1, 1)
+            start = max(i, k + 2) * N
+            if start < COLS:
+                later(update, k, i, work, tri_ref, slice(start, COLS))
+            later(update, k, i, work, inv_ref, slice(0, (k + 1) * N))
+            later(update, k, i, left, left, everything)
+        if k == LAGS - 2:
+            for j in range(LAGS - 1):
+                later(project, slice(0, (LAGS - 1) * N), j)
+    while waiting:
+        between()
+    for j in range(LAGS - 1):
+        project(block(LAGS - 1), j)
+    project(everything, LAGS - 1)
 
 
 def shifted(value, steps):
@@ -394,10 +423,14 @@
     params = pltpu.CompilerParams(vmem_limit_bytes=VMEM_LIMIT)
     head, rear = pl.pallas_call(
         carve_kernel,
-        out_shape=[jax.ShapeDtypeStruct((DOWN + 8, N), jnp.float32), jax.ShapeDtypeStruct((UP, N), jnp.float32)],
+        out_shape=[jax.ShapeDtypeStruct((DOWN + 16, N), jnp.float32), jax.ShapeDtypeStruct((UP, N), jnp.float32)],
         in_specs=[pl.BlockSpec(memory_space=pltpu.HBM)],
-        out_specs=[vmem, vmem],
-        scratch_shapes=[pltpu.SemaphoreType.DMA((2,))],
+        out_specs=[pl.BlockSpec(memory_space=pltpu.HBM)] * 2,
+        scratch_shapes=[
+            pltpu.VMEM((DOWN + 16 + UP, N), jnp.float32),
+            pltpu.SemaphoreType.DMA((2 * CARVE,)),
+            pltpu.SemaphoreType.DMA((2 * CARVE,)),
+        ],
         compiler_params=pltpu.CompilerParams(vmem_limit_bytes=62 * 2**20),
         name="carve",
     )(record)
@@ -448,7 +481,7 @@
             scratch_shapes=[
                 pltpu.VMEM((2, GRAM_SIDE * N, N), jnp.float32),
                 pltpu.VMEM((2, CROSS_SIDE * N, N), jnp.float32),
-                pltpu.VMEM((LAGS, N, COLS), jnp.float32),
+                pltpu.VMEM((COLS, COLS), jnp.float32),
                 pltpu.VMEM((COLS, COLS), jnp.float32),
                 pltpu.VMEM((COLS, COLS), jnp.float32),
             ],

time: 124 us -> 121 us (0.976)
  Pallas kernels: 33.2 us -> 30 us
    pallas_call x1, Pallas kernels: 22.4 us -> 19.7 us  [on_device(): pl.pallas_call(functools.partial(tail_kernel, 1.0 / last_row), out_shape=...]
where the time goes in v5:
time: 121 us; the launch traced here: 120 us
  blocking collectives  50.7 us (42%)
  Pallas kernels  30 us (25%)
  waiting for transfers between devices  20.2 us (17%)
  starting transfers between devices  16.8 us (14%)
  local copies, waits for them, and re-layouts  1.59 us (1%)
    all_to_all x3, blocking collectives, trade(): return lax.all_to_all(value, AXES, 0, 0, axis_index_groups=groups)  50.7 us
    pallas_call x1, Pallas kernels, on_device(): pl.pallas_call(functools.partial(tail_kernel, 1.0 / last_row), out_shape=...  19.7 us
    ppermute x2, waiting for transfers between devices, shifted(): lax.ppermute(value, AXES, [(source, source + steps) for source in range(l...  15.8 us
    ppermute x2, starting transfers between devices, shifted(): lax.ppermute(value, AXES, [(source, source + steps) for source in range(l...  13 us
    ppermute x2, waiting for transfers between devices, across_cores(): lax.ppermute(value, 'grp', [(source, source ^ 1) for source in range(coun...  4.37 us
    pallas_call x1, Pallas kernels, averaged_blocks(): pl.pallas_call(local_kernel, out_shape=[jax.ShapeDtypeStruct((BLOCKS, N,...  4.35 us
    ppermute x2, starting transfers between devices, across_cores(): lax.ppermute(value, 'grp', [(source, source ^ 1) for source in range(coun...  3.77 us
    pallas_call x1, Pallas kernels, averaged_blocks(): pl.pallas_call(halo_kernel, out_shape=[side, side], in_specs=[smem, vmem,...  3.64 us
  transfers between devices with their start and end apart: 4, of which 3 were waited for; matrix products, arithmetic and copies ran while one was open for 0% of the time, Pallas kernels for 4%

profile of v5, /device:TPU:1, one launch (start us, length us, event | category | flops | bytes accessed | tf_op | source)
XLA Modules:
  0.0 120.2 jit_solution(11812784196597485212)
XLA Ops:
  0.6 2.2 %carve.1 = (f32[1680,128]{1,0:T(8,128)}, f32[1408,128]{1,0:T(8,128)}) custom-call(f32[4096,128]{1,0:T(8,128)} %rec_ref.3), custom_call_target="tpu_custom_call" | custom-call | tf_op jit(solution)/shard_map/carve/pallas_call | solution.py:424
  2.9 11.1 %collective-permute-start = (f32[1680,128]{1,0:T(8,128)}, f32[1680,128]{1,0:T(8,128)S(1)}, u32[]{:S(2)}, u32[]{:S(2)}) collective-permute-start(f32[1680,128]{1,0:T(8,128)} %get-tuple-element.10), channel_id=1, source_target_pairs={{1,0},{2,1},{3,2},{4,3},{5,4},{6,5},{7,6},{8,7},{9,8},{10,9},{11,1... | collective-permute-start | bytes 2580488 | tf_op jit(solution)/shard_map/ppermute | solution.py:373
  13.9 1.9 %collective-permute-start.1 = (f32[1408,128]{1,0:T(8,128)}, f32[1408,128]{1,0:T(8,128)S(1)}, u32[]{:S(2)}, u32[]{:S(2)}) collective-permute-start(f32[1408,128]{1,0:T(8,128)} %get-tuple-element.11), channel_id=1, source_target_pairs={{0,1},{1,2},{2,3},{3,4},{4,5},{5,6},{6,7},{7,8},{8,9},{9,10},{10,1... | collective-permute-start | bytes 2162696 | tf_op jit(solution)/shard_map/ppermute | solution.py:373
  15.9 0.1 pad_add_fusion.edge_ref
  16.0 0.0 copy-start
  16.0 1.6 %copy-done = f32[4096,128]{1,0:T(8,128)S(1)} copy-done((f32[4096,128]{1,0:T(8,128)S(1)}, f32[4096,128]{1,0:T(8,128)}, u32[]{:S(2)}) %copy-start) | copy-done | bytes 2097176
  17.5 4.4 %local_products.1 = (f32[26,128,128]{2,1,0:T(8,128)S(1)}, bf16[4096,512]{1,0:T(8,128)(2,1)S(1)}) custom-call(s32[3]{0:T(128)S(1)} %pad_add_fusion.edge_ref, f32[4096,128]{1,0:T(8,128)S(1)} %copy-done), custom_call_target="tpu_custom_call" | custom-call | flops 4000000000 | bytes 8388608 | tf_op jit(solution)/shard_map/local_products/pallas_call | solution.py:438
  21.9 15.8 %collective-permute-done.1.up_ref = f32[1408,128]{1,0:T(8,128)S(1)} collective-permute-done((f32[1408,128]{1,0:T(8,128)}, f32[1408,128]{1,0:T(8,128)S(1)}, u32[]{:S(2)}, u32[]{:S(2)}) %collective-permute-start.1) | collective-permute-done | bytes 720928 | tf_op jit(solution)/shard_map/ppermute | solution.py:373
  37.7 0.0 collective-permute-done.down_ref
  37.8 3.6 %halo_products.1 = (f32[16,104,128]{2,1,0:T(8,128)S(1)}, f32[16,104,128]{2,1,0:T(8,128)S(1)}) custom-call(s32[3]{0:T(128)S(1)} %pad_add_fusion.edge_ref, f32[26,128,128]{2,1,0:T(8,128)S(1)} %get-tuple-element.8.acc_ref, bf16[4096,512]{1,0:T(8,128)(2,1)S(1)} %get-tuple-element.9.split_ref, f32[1680,128]{1,0:T(8,128)S(1)} %collective-permute-done.down_ref, ...), custom_call_target="tpu_custom_call" | custom-call | flops 3000000000 | bytes 9437184 | tf_op jit(solution)/shard_map/halo_products/pallas_call | solution.py:453
  41.4 0.1 collective-permute-start.2
  41.5 2.4 %collective-permute-done.2 = f32[16,104,128]{2,1,0:T(8,128)S(1)} collective-permute-done((f32[16,104,128]{2,1,0:T(8,128)S(1)}, f32[16,104,128]{2,1,0:T(8,128)S(1)}, u32[]{:S(2)}, u32[]{:S(2)}) %collective-permute-start.2) | collective-permute-done | bytes 852000 | tf_op jit(solution)/shard_map/ppermute | solution.py:395
  43.9 0.1 add.12
  44.0 19.0 %all_to_all.15.in_ref = f32[16,104,128]{2,1,0:T(8,128)S(1)} all-to-all(f32[16,104,128]{2,1,0:T(8,128)S(1)} %add.12), channel_id=1, replica_groups={{0,1,2,3,64,65,66,67,128,129,130,131,192,193,194,195},{4,5,6,7,68,69,70..., dimensions={0} | all-to-all | bytes 1703936 | tf_op jit(solution)/shard_map/all_to_all | solution.py:379
  63.0 0.1 add_and_repeat.2
  63.0 16.1 %all_to_all.16.in_ref = f32[8,104,128]{2,1,0:T(8,128)S(1)} all-to-all(f32[8,104,128]{2,1,0:T(8,128)S(1)} %add_and_repeat.2), channel_id=1, replica_groups={{0,4,8,12,16,20,24,28},{1,5,9,13,17,21,25,29},{2,6,10,14,18,22,26,30},{..., dimensions={0} | all-to-all | bytes 851968 | tf_op jit(solution)/shard_map/all_to_all | solution.py:379
  79.1 0.1 add_and_repeat.3
  79.2 15.6 %all_to_all.17.mine_ref = f32[16,104,128]{2,1,0:T(8,128)S(1)} all-to-all(f32[16,104,128]{2,1,0:T(8,128)S(1)} %add_and_repeat.3), channel_id=1, replica_groups={{0,1,2,3,64,65,66,67,128,129,130,131,192,193,194,195},{4,5,6,7,68,69,70..., dimensions={0} | all-to-all | bytes 1703936 | tf_op jit(solution)/shard_map/all_to_all | solution.py:379
  94.8 3.7 %collective-permute-start.3 = (f32[16,104,128]{2,1,0:T(8,128)S(1)}, f32[16,104,128]{2,1,0:T(8,128)S(1)}, u32[]{:S(2)}, u32[]{:S(2)}) collective-permute-start(f32[16,104,128]{2,1,0:T(8,128)S(1)} %all_to_all.17.mine_ref), channel_id=1, source_target_pairs={{0,32},{32,0},{64,96},{96,64},{128,160},{160,128},{192,224},{224,1... | collective-permute-start | bytes 2555912 | tf_op jit(solution)/shard_map/ppermute | solution.py:395
  98.5 2.0 %collective-permute-done.3.other_ref = f32[16,104,128]{2,1,0:T(8,128)S(1)} collective-permute-done((f32[16,104,128]{2,1,0:T(8,128)S(1)}, f32[16,104,128]{2,1,0:T(8,128)S(1)}, u32[]{:S(2)}, u32[]{:S(2)}) %collective-permute-start.3) | collective-permute-done | bytes 852000 | tf_op jit(solution)/shard_map/ppermute | solution.py:395
  100.5 19.7 %factor_and_solve.1 = (f32[512,512]{1,0:T(8,128)}, f32[512,512]{1,0:T(8,128)}) custom-call(s32[3]{0:T(128)S(1)} %pad_add_fusion.edge_ref, f32[16,104,128]{2,1,0:T(8,128)S(1)} %all_to_all.17.mine_ref, f32[16,104,128]{2,1,0:T(8,128)S(1)} %collective-permute-done.3.other_ref), custom_call_target="tpu_custom_call" | custom-call | tf_op jit(solution)/shard_map/factor_and_solve/pallas_call | solution.py:476
Async XLA Ops:
  2.9 34.9 %collective-permute-start = (f32[1680,128]{1,0:T(8,128)}, f32[1680,128]{1,0:T(8,128)S(1)}, u32[]{:S(2)}, u32[]{:S(2)}) collective-permute-start(f32[1680,128]{1,0:T(8,128)} %get-tuple-element.10), channel_id=1, source_target_pairs={{1,0},{2,1},{3,2},{4,3},{5,4},{6,5},{7,6},{8,7},{9,8},{10,9},{11,1... | collective-permute-start | bytes 2580488 | tf_op jit(solution)/shard_map/ppermute | solution.py:373
  13.9 23.8 %collective-permute-start.1 = (f32[1408,128]{1,0:T(8,128)}, f32[1408,128]{1,0:T(8,128)S(1)}, u32[]{:S(2)}, u32[]{:S(2)}) collective-permute-start(f32[1408,128]{1,0:T(8,128)} %get-tuple-element.11), channel_id=1, source_target_pairs={{0,1},{1,2},{2,3},{3,4},{4,5},{5,6},{6,7},{7,8},{8,9},{9,10},{10,1... | collective-permute-start | bytes 2162696 | tf_op jit(solution)/shard_map/ppermute | solution.py:373
  16.0 1.6 %copy-start = (f32[4096,128]{1,0:T(8,128)S(1)}, f32[4096,128]{1,0:T(8,128)}, u32[]{:S(2)}) copy-start(f32[4096,128]{1,0:T(8,128)} %rec_ref.3) | copy-start | bytes 6291460
  41.4 2.5 %collective-permute-start.2 = (f32[16,104,128]{2,1,0:T(8,128)S(1)}, f32[16,104,128]{2,1,0:T(8,128)S(1)}, u32[]{:S(2)}, u32[]{:S(2)}) collective-permute-start(f32[16,104,128]{2,1,0:T(8,128)S(1)} %get-tuple-element.13), channel_id=1, source_target_pairs={{0,32},{32,0},{64,96},{96,64},{128,160},{160,128},{192,224},{224,1... | collective-permute-start | bytes 2555912 | tf_op jit(solution)/shard_map/ppermute | solution.py:395
  94.8 5.7 %collective-permute-start.3 = (f32[16,104,128]{2,1,0:T(8,128)S(1)}, f32[16,104,128]{2,1,0:T(8,128)S(1)}, u32[]{:S(2)}, u32[]{:S(2)}) collective-permute-start(f32[16,104,128]{2,1,0:T(8,128)S(1)} %all_to_all.17.mine_ref), channel_id=1, source_target_pairs={{0,32},{32,0},{64,96},{96,64},{128,160},{160,128},{192,224},{224,1... | collective-permute-start | bytes 2555912 | tf_op jit(solution)/shard_map/ppermute | solution.py:395

commit v6 on v5

--- a/solution.py
+++ b/solution.py
@@ -11,7 +11,7 @@
 DELAY = 1024
 N = 128
 COLS = LAGS * N
-CUT = 640
+CUT = 608
 DOWN, UP = DELAY + CUT, 2 * DELAY - CUT
 AXES = ("grp", "span")
 HIGHEST = lax.Precision.HIGHEST
@@ -217,6 +217,10 @@
     return jnp.broadcast_to(value[t : t + 1, :], (n, N))
 
 
+def whole(ref, slot, row):
+    return jnp.broadcast_to(ref[slot, row : row + 1, :], (8, N))
+
+
 def three(value):
     high = value.astype(jnp.bfloat16)
     rest = value - high.astype(jnp.float32)
@@ -234,43 +238,50 @@
     )
 
 
-def factor(matrix, between):
+def factor(matrix, between, spread):
     sub = lax.broadcasted_iota(jnp.int32, (8, N), 0)
     lane = lax.broadcasted_iota(jnp.int32, (8, N), 1)
     rows = [matrix[r : r + 8] for r in range(0, N, 8)]
     uppers, inverses = [], []
     for k in range(len(rows)):
         first = 8 * k
-        old, inside = lane < first + 8, (lane >= first) & (lane < first + 8)
-        top = rows[k]
-        grown = jnp.where(lane < first, top, 0.0) + jnp.where(lane == sub + first, 1.0, 0.0)
-        cols = [lanes(top, first + t) for t in range(8)]
+        inside = (lane >= first) & (lane < first + 8)
+        at = [lane == first + t for t in range(8)]
+        cols = [lanes(rows[k], first + t) for t in range(8)]
+        held = k % 2
+        for u in range(8):
+            spread[held, 8 * u : 8 * u + 8] = cols[u]
+        spread[held, 64:72] = jnp.where(inside, 0.0, rows[k])
+        corner = [[whole(spread, held, 8 * u + t) if u >= t else None for u in range(8)] for t in range(8)]
+        top = [jnp.where(at[t], 1.0, whole(spread, held, 64 + t)) for t in range(8)]
         others = list(range(k + 1, k - k % GROUP + GROUP))
         below = {v: [lanes(rows[v], first + t) for t in range(8)] for v in others}
         for v in others:
             rows[v] = jnp.where(inside, 0.0, rows[v])
-        pivots = jnp.zeros((8, N), jnp.float32)
+        pivots, both, diagonal = jnp.zeros((8, N), jnp.float32), jnp.zeros((8, N), jnp.float32), jnp.zeros((8, N), jnp.float32)
         for t in range(8):
-            pivot = line(cols[t], t, 8)
-            recip = 1.0 / pivot
-            mult = jnp.where(sub > t, cols[t] * recip, 0.0)
-            entries = [line(cols[u], t, 8) for u in range(t + 1, 8)]
-            top_line, grown_line = line(top, t, 8), line(grown, t, 8)
-            for u, entry in zip(range(t + 1, 8), entries):
-                cols[u] = cols[u] - mult * entry
-            pivots = jnp.where(sub == t, pivot, pivots)
-            if others:
-                both = jnp.where(old, grown_line, top_line)
+            recip = 1.0 / corner[t][t]
+            for u in range(t + 1, 8):
+                mult = corner[t][u] * recip
+                for w in range(u, 8):
+                    corner[u][w] = corner[u][w] - mult * corner[t][w]
+                top[u] = top[u] - mult * top[t]
             for v in others:
-                mult_below = below[v][t] * recip
-                for u, entry in zip(range(t + 1, 8), entries):
-                    below[v][u] = below[v][u] - mult_below * entry
-                rows[v] = rows[v] - mult_below * both
-            top = top - mult * top_line
-            grown = grown - mult * grown_line
+                mult = below[v][t] * recip
+                for u in range(t + 1, 8):
+                    below[v][u] = below[v][u] - mult * corner[t][u]
+                rows[v] = rows[v] - mult * top[t]
+            own = jnp.zeros((8, N), jnp.float32)
+            for u in range(t, 8):
+                own = jnp.where(at[u], corner[t][u], own)
+            here = sub == t
+            pivots = jnp.where(here, corner[t][t], pivots)
+            both = jnp.where(here, top[t], both)
+            diagonal = jnp.where(here, own, diagonal)
         root = lax.rsqrt(pivots)
-        uppers.append(jnp.where(lane >= sub + first, top * root, 0.0))
-        inverses.append(grown * root)
+        both = both * root
+        uppers.append(jnp.where(lane >= first + 8, both, diagonal * root))
+        inverses.append(jnp.where(lane < first + 8, both, 0.0))
         between()
         end = k + 1
         if end % GROUP == 0 and end < len(rows):
@@ -284,7 +295,7 @@
     return jnp.concatenate(uppers, 0), jnp.concatenate(inverses, 0)
 
 
-def tail_kernel(scale, edge_ref, mine_ref, other_ref, tri_ref, op_ref, gram, cross, work, inv, left):
+def tail_kernel(scale, edge_ref, mine_ref, other_ref, tri_ref, op_ref, gram, cross, work, inv, left, spread):
     core = edge_ref[2]
     few = gram.shape[1] // mine_ref.shape[0]
     many = cross.shape[1] // mine_ref.shape[0]
@@ -292,10 +303,10 @@
         for m in range(ref.shape[0]):
             gram[side, m * few : (m + 1) * few] = ref[m, :few] * scale
             cross[side, m * many : (m + 1) * many] = ref[m, few:] * scale
-    factor_and_solve(gram, cross, tri_ref, op_ref, inv, work, left)
-
-
-def factor_and_solve(gram, cross, tri_ref, op_ref, inv_ref, work, left):
+    factor_and_solve(gram, cross, tri_ref, op_ref, inv, work, left, spread)
+
+
+def factor_and_solve(gram, cross, tri_ref, op_ref, inv_ref, work, left, spread):
     def block(k):
         return slice(k * N, (k + 1) * N)
 
@@ -338,7 +349,7 @@
             later(fetch, i, j)
     everything = slice(0, COLS)
     for k in range(LAGS):
-        upper, inverse = factor(work[block(k), block(k)], between)
+        upper, inverse = factor(work[block(k), block(k)], between, spread)
         while waiting:
             between()
         tri_ref[block(k), block(k)] = upper
@@ -484,6 +495,7 @@
                 pltpu.VMEM((COLS, COLS), jnp.float32),
                 pltpu.VMEM((COLS, COLS), jnp.float32),
                 pltpu.VMEM((COLS, COLS), jnp.float32),
+                pltpu.VMEM((2, 72, N), jnp.float32),
             ],
             compiler_params=pltpu.CompilerParams(vmem_limit_bytes=VMEM_LIMIT),
             name="factor_and_solve",

time: 121 us -> 119 us (0.983)
  Pallas kernels: 30 us -> 28.5 us
    pallas_call x1, Pallas kernels: 19.7 us -> 18.1 us  [on_device(): pl.pallas_call(functools.partial(tail_kernel, 1.0 / last_row), out_shape=...]
where the time goes in v6:
time: 119 us
  blocking collectives  50.7 us (43%)
  Pallas kernels  28.5 us (24%)
  waiting for transfers between devices  20.6 us (17%)
  starting transfers between devices  16.8 us (14%)
  local copies, waits for them, and re-layouts  1.59 us (1%)
    all_to_all x3, blocking collectives, trade(): return lax.all_to_all(value, AXES, 0, 0, axis_index_groups=groups)  50.7 us
    pallas_call x1, Pallas kernels, on_device(): pl.pallas_call(functools.partial(tail_kernel, 1.0 / last_row), out_shape=...  18.1 us
    ppermute x2, waiting for transfers between devices, shifted(): lax.ppermute(value, AXES, [(source, source + steps) for source in range(l...  16.2 us
    ppermute x2, starting transfers between devices, shifted(): lax.ppermute(value, AXES, [(source, source + steps) for source in range(l...  13 us
    ppermute x2, waiting for transfers between devices, across_cores(): lax.ppermute(value, 'grp', [(source, source ^ 1) for source in range(coun...  4.37 us
    pallas_call x1, Pallas kernels, averaged_blocks(): pl.pallas_call(local_kernel, out_shape=[jax.ShapeDtypeStruct((BLOCKS, N,...  4.35 us
    ppermute x2, starting transfers between devices, across_cores(): lax.ppermute(value, 'grp', [(source, source ^ 1) for source in range(coun...  3.77 us
    pallas_call x1, Pallas kernels, averaged_blocks(): pl.pallas_call(halo_kernel, out_shape=[side, side], in_specs=[smem, vmem,...  3.64 us
  transfers between devices with their start and end apart: 4, of which 3 were waited for; matrix products, arithmetic and copies ran while one was open for 0% of the time, Pallas kernels for 4%

profile of v6, /device:TPU:1, one launch (start us, length us, event | category | flops | bytes accessed | tf_op | source)
XLA Modules:
  0.0 119.0 jit_solution(13751584554282333880)
XLA Ops:
  0.6 2.2 %carve.1 = (f32[1648,128]{1,0:T(8,128)}, f32[1440,128]{1,0:T(8,128)}) custom-call(f32[4096,128]{1,0:T(8,128)} %rec_ref.3), custom_call_target="tpu_custom_call" | custom-call | tf_op jit(solution)/shard_map/carve/pallas_call | solution.py:435
  2.9 11.1 %collective-permute-start = (f32[1648,128]{1,0:T(8,128)}, f32[1648,128]{1,0:T(8,128)S(1)}, u32[]{:S(2)}, u32[]{:S(2)}) collective-permute-start(f32[1648,128]{1,0:T(8,128)} %get-tuple-element.10), channel_id=1, source_target_pairs={{1,0},{2,1},{3,2},{4,3},{5,4},{6,5},{7,6},{8,7},{9,8},{10,9},{11,1... | collective-permute-start | bytes 2531336 | tf_op jit(solution)/shard_map/ppermute | solution.py:384
  13.9 1.9 %collective-permute-start.1 = (f32[1440,128]{1,0:T(8,128)}, f32[1440,128]{1,0:T(8,128)S(1)}, u32[]{:S(2)}, u32[]{:S(2)}) collective-permute-start(f32[1440,128]{1,0:T(8,128)} %get-tuple-element.11), channel_id=1, source_target_pairs={{0,1},{1,2},{2,3},{3,4},{4,5},{5,6},{6,7},{7,8},{8,9},{9,10},{10,1... | collective-permute-start | bytes 2211848 | tf_op jit(solution)/shard_map/ppermute | solution.py:384
  15.9 0.1 pad_add_fusion.edge_ref
  15.9 0.0 copy-start
  16.0 1.6 %copy-done = f32[4096,128]{1,0:T(8,128)S(1)} copy-done((f32[4096,128]{1,0:T(8,128)S(1)}, f32[4096,128]{1,0:T(8,128)}, u32[]{:S(2)}) %copy-start) | copy-done | bytes 2097176
  17.5 4.4 %local_products.1 = (f32[26,128,128]{2,1,0:T(8,128)S(1)}, bf16[4096,512]{1,0:T(8,128)(2,1)S(1)}) custom-call(s32[3]{0:T(128)S(1)} %pad_add_fusion.edge_ref, f32[4096,128]{1,0:T(8,128)S(1)} %copy-done), custom_call_target="tpu_custom_call" | custom-call | flops 4000000000 | bytes 8388608 | tf_op jit(solution)/shard_map/local_products/pallas_call | solution.py:449
  21.9 16.2 %collective-permute-done.1.up_ref = f32[1440,128]{1,0:T(8,128)S(1)} collective-permute-done((f32[1440,128]{1,0:T(8,128)}, f32[1440,128]{1,0:T(8,128)S(1)}, u32[]{:S(2)}, u32[]{:S(2)}) %collective-permute-start.1) | collective-permute-done | bytes 737312 | tf_op jit(solution)/shard_map/ppermute | solution.py:384
  38.1 0.0 collective-permute-done.down_ref
  38.1 3.6 %halo_products.1 = (f32[16,104,128]{2,1,0:T(8,128)S(1)}, f32[16,104,128]{2,1,0:T(8,128)S(1)}) custom-call(s32[3]{0:T(128)S(1)} %pad_add_fusion.edge_ref, f32[26,128,128]{2,1,0:T(8,128)S(1)} %get-tuple-element.8.acc_ref, bf16[4096,512]{1,0:T(8,128)(2,1)S(1)} %get-tuple-element.9.split_ref, f32[1648,128]{1,0:T(8,128)S(1)} %collective-permute-done.down_ref, ...), custom_call_target="tpu_custom_call" | custom-call | flops 3000000000 | bytes 9437184 | tf_op jit(solution)/shard_map/halo_products/pallas_call | solution.py:464
  41.7 0.1 collective-permute-start.2
  41.8 2.4 %collective-permute-done.2 = f32[16,104,128]{2,1,0:T(8,128)S(1)} collective-permute-done((f32[16,104,128]{2,1,0:T(8,128)S(1)}, f32[16,104,128]{2,1,0:T(8,128)S(1)}, u32[]{:S(2)}, u32[]{:S(2)}) %collective-permute-start.2) | collective-permute-done | bytes 852000 | tf_op jit(solution)/shard_map/ppermute | solution.py:406
  44.2 0.1 add.12
  44.3 19.0 %all_to_all.15.in_ref = f32[16,104,128]{2,1,0:T(8,128)S(1)} all-to-all(f32[16,104,128]{2,1,0:T(8,128)S(1)} %add.12), channel_id=1, replica_groups={{0,1,2,3,64,65,66,67,128,129,130,131,192,193,194,195},{4,5,6,7,68,69,70..., dimensions={0} | all-to-all | bytes 1703936 | tf_op jit(solution)/shard_map/all_to_all | solution.py:390
  63.3 0.1 add_and_repeat.2
  63.4 16.1 %all_to_all.16.in_ref = f32[8,104,128]{2,1,0:T(8,128)S(1)} all-to-all(f32[8,104,128]{2,1,0:T(8,128)S(1)} %add_and_repeat.2), channel_id=1, replica_groups={{0,4,8,12,16,20,24,28},{1,5,9,13,17,21,25,29},{2,6,10,14,18,22,26,30},{..., dimensions={0} | all-to-all | bytes 851968 | tf_op jit(solution)/shard_map/all_to_all | solution.py:390
  79.5 0.1 add_and_repeat.3
  79.6 15.6 %all_to_all.17.mine_ref = f32[16,104,128]{2,1,0:T(8,128)S(1)} all-to-all(f32[16,104,128]{2,1,0:T(8,128)S(1)} %add_and_repeat.3), channel_id=1, replica_groups={{0,1,2,3,64,65,66,67,128,129,130,131,192,193,194,195},{4,5,6,7,68,69,70..., dimensions={0} | all-to-all | bytes 1703936 | tf_op jit(solution)/shard_map/all_to_all | solution.py:390
  95.2 3.7 %collective-permute-start.3 = (f32[16,104,128]{2,1,0:T(8,128)S(1)}, f32[16,104,128]{2,1,0:T(8,128)S(1)}, u32[]{:S(2)}, u32[]{:S(2)}) collective-permute-start(f32[16,104,128]{2,1,0:T(8,128)S(1)} %all_to_all.17.mine_ref), channel_id=1, source_target_pairs={{0,32},{32,0},{64,96},{96,64},{128,160},{160,128},{192,224},{224,1... | collective-permute-start | bytes 2555912 | tf_op jit(solution)/shard_map/ppermute | solution.py:406
  98.9 2.0 %collective-permute-done.3.other_ref = f32[16,104,128]{2,1,0:T(8,128)S(1)} collective-permute-done((f32[16,104,128]{2,1,0:T(8,128)S(1)}, f32[16,104,128]{2,1,0:T(8,128)S(1)}, u32[]{:S(2)}, u32[]{:S(2)}) %collective-permute-start.3) | collective-permute-done | bytes 852000 | tf_op jit(solution)/shard_map/ppermute | solution.py:406
  100.9 18.1 %factor_and_solve.1 = (f32[512,512]{1,0:T(8,128)}, f32[512,512]{1,0:T(8,128)}) custom-call(s32[3]{0:T(128)S(1)} %pad_add_fusion.edge_ref, f32[16,104,128]{2,1,0:T(8,128)S(1)} %all_to_all.17.mine_ref, f32[16,104,128]{2,1,0:T(8,128)S(1)} %collective-permute-done.3.other_ref), custom_call_target="tpu_custom_call" | custom-call | tf_op jit(solution)/shard_map/factor_and_solve/pallas_call | solution.py:487
Async XLA Ops:
  2.9 35.2 %collective-permute-start = (f32[1648,128]{1,0:T(8,128)}, f32[1648,128]{1,0:T(8,128)S(1)}, u32[]{:S(2)}, u32[]{:S(2)}) collective-permute-start(f32[1648,128]{1,0:T(8,128)} %get-tuple-element.10), channel_id=1, source_target_pairs={{1,0},{2,1},{3,2},{4,3},{5,4},{6,5},{7,6},{8,7},{9,8},{10,9},{11,1... | collective-permute-start | bytes 2531336 | tf_op jit(solution)/shard_map/ppermute | solution.py:384
  13.9 24.2 %collective-permute-start.1 = (f32[1440,128]{1,0:T(8,128)}, f32[1440,128]{1,0:T(8,128)S(1)}, u32[]{:S(2)}, u32[]{:S(2)}) collective-permute-start(f32[1440,128]{1,0:T(8,128)} %get-tuple-element.11), channel_id=1, source_target_pairs={{0,1},{1,2},{2,3},{3,4},{4,5},{5,6},{6,7},{7,8},{8,9},{9,10},{10,1... | collective-permute-start | bytes 2211848 | tf_op jit(solution)/shard_map/ppermute | solution.py:384
  15.9 1.6 %copy-start = (f32[4096,128]{1,0:T(8,128)S(1)}, f32[4096,128]{1,0:T(8,128)}, u32[]{:S(2)}) copy-start(f32[4096,128]{1,0:T(8,128)} %rec_ref.3) | copy-start | bytes 6291460
  41.7 2.5 %collective-permute-start.2 = (f32[16,104,128]{2,1,0:T(8,128)S(1)}, f32[16,104,128]{2,1,0:T(8,128)S(1)}, u32[]{:S(2)}, u32[]{:S(2)}) collective-permute-start(f32[16,104,128]{2,1,0:T(8,128)S(1)} %get-tuple-element.13), channel_id=1, source_target_pairs={{0,32},{32,0},{64,96},{96,64},{128,160},{160,128},{192,224},{224,1... | collective-permute-start | bytes 2555912 | tf_op jit(solution)/shard_map/ppermute | solution.py:406
  95.2 5.7 %collective-permute-start.3 = (f32[16,104,128]{2,1,0:T(8,128)S(1)}, f32[16,104,128]{2,1,0:T(8,128)S(1)}, u32[]{:S(2)}, u32[]{:S(2)}) collective-permute-start(f32[16,104,128]{2,1,0:T(8,128)S(1)} %all_to_all.17.mine_ref), channel_id=1, source_target_pairs={{0,32},{32,0},{64,96},{96,64},{128,160},{160,128},{192,224},{224,1... | collective-permute-start | bytes 2555912 | tf_op jit(solution)/shard_map/ppermute | solution.py:406

commit v7 on v6

--- a/solution.py
+++ b/solution.py
@@ -24,7 +24,7 @@
 GRAM_SIDE, CROSS_SIDE = len(GRAM) // 2, len(CROSS) // 2
 CHIPS_X = 4
 CARVE = 2
-GROUP = 4
+GROUP = 8
 
 
 def exact(left, right, dims):
@@ -334,12 +334,21 @@
     def solve_side(k, inverse, target, source, columns):
         target[block(k), columns] = stacked(inverse, source[block(k), columns], 1, 0)
 
-    def update(k, i, target, source, columns):
-        target[block(i), columns] -= stacked(tri_ref[block(k), block(i)], source[block(k), columns], 0, 0)
-
-    def project(rows, j):
+    def update(k, i, *triples):
+        right = jnp.concatenate([source[block(k), columns] for _, source, columns in triples], 1)
+        change, start = stacked(tri_ref[block(k), block(i)].T, right, 1, 0), 0
+        for target, _, columns in triples:
+            stop = start + columns.stop - columns.start
+            target[block(i), columns] -= change[:, start:stop]
+            start = stop
+
+    def project(j):
         known = slice(0, (j + 1) * N)
-        op_ref[rows, block(j)] = stacked(left[rows, known], inv_ref[block(j), known], 1, 1)
+        op_ref[:, block(j)] = stacked(left[:, known], inv_ref[block(j), known], 1, 1)
+
+    def project_last():
+        known = slice(0, (LAGS - 1) * N)
+        op_ref[:, block(LAGS - 1)] = left[:, block(LAGS - 1)] + stacked(left[:, known], work[block(LAGS - 1), known], 1, 1)
 
     def later(function, *args):
         waiting.append(functools.partial(function, *args))
@@ -353,29 +362,28 @@
         while waiting:
             between()
         tri_ref[block(k), block(k)] = upper
+        if k == LAGS - 1:
+            break
         inv_ref[block(k), block(k)] = inverse
-        if k + 1 < LAGS:
-            solve_side(k, inverse, tri_ref, work, block(k + 1))
-            update(k, k + 1, work, tri_ref, block(k + 1))
+        solve_side(k, inverse, tri_ref, work, block(k + 1))
+        update(k, k + 1, (work, tri_ref, block(k + 1)))
         if k + 2 < LAGS:
             later(solve_side, k, inverse, tri_ref, work, slice((k + 2) * N, COLS))
         if k:
             later(solve_side, k, inverse, inv_ref, work, slice(0, k * N))
         later(solve_side, k, inverse, left, left, everything)
         for i in range(k + 1, LAGS):
+            triples = [(work, inv_ref, slice(0, (k + 1) * N)), (left, left, everything)]
             start = max(i, k + 2) * N
             if start < COLS:
-                later(update, k, i, work, tri_ref, slice(start, COLS))
-            later(update, k, i, work, inv_ref, slice(0, (k + 1) * N))
-            later(update, k, i, left, left, everything)
+                triples.append((work, tri_ref, slice(start, COLS)))
+            later(update, k, i, *triples)
         if k == LAGS - 2:
             for j in range(LAGS - 1):
-                later(project, slice(0, (LAGS - 1) * N), j)
-    while waiting:
-        between()
-    for j in range(LAGS - 1):
-        project(block(LAGS - 1), j)
-    project(everything, LAGS - 1)
+                later(project, j)
+            later(project_last)
+    op_ref[:, block(k)] = stacked(op_ref[:, block(k)], inverse, 1, 1)
+    op_ref[block(k), :] = stacked(inverse, op_ref[block(k), :], 1, 0)
 
 
 def shifted(value, steps):

time: 119 us -> 119 us (level)
  no operation moved by 1% of the time
where the time goes in v7:
time: 119 us; the launch traced here: 118 us
  blocking collectives  50.7 us (43%)
  Pallas kernels  27.8 us (23%)
  waiting for transfers between devices  20.6 us (17%)
  starting transfers between devices  16.8 us (14%)
  local copies, waits for them, and re-layouts  1.59 us (1%)
    all_to_all x3, blocking collectives, trade(): return lax.all_to_all(value, AXES, 0, 0, axis_index_groups=groups)  50.7 us
    pallas_call x1, Pallas kernels, on_device(): pl.pallas_call(functools.partial(tail_kernel, 1.0 / last_row), out_shape=...  17.5 us
    ppermute x2, waiting for transfers between devices, shifted(): lax.ppermute(value, AXES, [(source, source + steps) for source in range(l...  16.2 us
    ppermute x2, starting transfers between devices, shifted(): lax.ppermute(value, AXES, [(source, source + steps) for source in range(l...  13 us
    ppermute x2, waiting for transfers between devices, across_cores(): lax.ppermute(value, 'grp', [(source, source ^ 1) for source in range(coun...  4.37 us
    pallas_call x1, Pallas kernels, averaged_blocks(): pl.pallas_call(local_kernel, out_shape=[jax.ShapeDtypeStruct((BLOCKS, N,...  4.35 us
    ppermute x2, starting transfers between devices, across_cores(): lax.ppermute(value, 'grp', [(source, source ^ 1) for source in range(coun...  3.77 us
    pallas_call x1, Pallas kernels, averaged_blocks(): pl.pallas_call(halo_kernel, out_shape=[side, side], in_specs=[smem, vmem,...  3.64 us
  transfers between devices with their start and end apart: 4, of which 3 were waited for; matrix products, arithmetic and copies ran while one was open for 0% of the time, Pallas kernels for 4%

profile of v7, /device:TPU:1, one launch (start us, length us, event | category | flops | bytes accessed | tf_op | source)
XLA Modules:
  0.0 118.3 jit_solution(5466983962614096993)
XLA Ops:
  0.6 2.2 %carve.1 = (f32[1648,128]{1,0:T(8,128)}, f32[1440,128]{1,0:T(8,128)}) custom-call(f32[4096,128]{1,0:T(8,128)} %rec_ref.3), custom_call_target="tpu_custom_call" | custom-call | tf_op jit(solution)/shard_map/carve/pallas_call | solution.py:443
  2.9 11.1 %collective-permute-start = (f32[1648,128]{1,0:T(8,128)}, f32[1648,128]{1,0:T(8,128)S(1)}, u32[]{:S(2)}, u32[]{:S(2)}) collective-permute-start(f32[1648,128]{1,0:T(8,128)} %get-tuple-element.10), channel_id=1, source_target_pairs={{1,0},{2,1},{3,2},{4,3},{5,4},{6,5},{7,6},{8,7},{9,8},{10,9},{11,1... | collective-permute-start | bytes 2531336 | tf_op jit(solution)/shard_map/ppermute | solution.py:392
  13.9 1.9 %collective-permute-start.1 = (f32[1440,128]{1,0:T(8,128)}, f32[1440,128]{1,0:T(8,128)S(1)}, u32[]{:S(2)}, u32[]{:S(2)}) collective-permute-start(f32[1440,128]{1,0:T(8,128)} %get-tuple-element.11), channel_id=1, source_target_pairs={{0,1},{1,2},{2,3},{3,4},{4,5},{5,6},{6,7},{7,8},{8,9},{9,10},{10,1... | collective-permute-start | bytes 2211848 | tf_op jit(solution)/shard_map/ppermute | solution.py:392
  15.9 0.1 pad_add_fusion.edge_ref
  15.9 0.0 copy-start
  16.0 1.6 %copy-done = f32[4096,128]{1,0:T(8,128)S(1)} copy-done((f32[4096,128]{1,0:T(8,128)S(1)}, f32[4096,128]{1,0:T(8,128)}, u32[]{:S(2)}) %copy-start) | copy-done | bytes 2097176
  17.5 4.4 %local_products.1 = (f32[26,128,128]{2,1,0:T(8,128)S(1)}, bf16[4096,512]{1,0:T(8,128)(2,1)S(1)}) custom-call(s32[3]{0:T(128)S(1)} %pad_add_fusion.edge_ref, f32[4096,128]{1,0:T(8,128)S(1)} %copy-done), custom_call_target="tpu_custom_call" | custom-call | flops 4000000000 | bytes 8388608 | tf_op jit(solution)/shard_map/local_products/pallas_call | solution.py:457
  21.9 16.2 %collective-permute-done.1.up_ref = f32[1440,128]{1,0:T(8,128)S(1)} collective-permute-done((f32[1440,128]{1,0:T(8,128)}, f32[1440,128]{1,0:T(8,128)S(1)}, u32[]{:S(2)}, u32[]{:S(2)}) %collective-permute-start.1) | collective-permute-done | bytes 737312 | tf_op jit(solution)/shard_map/ppermute | solution.py:392
  38.1 0.0 collective-permute-done.down_ref
  38.1 3.6 %halo_products.1 = (f32[16,104,128]{2,1,0:T(8,128)S(1)}, f32[16,104,128]{2,1,0:T(8,128)S(1)}) custom-call(s32[3]{0:T(128)S(1)} %pad_add_fusion.edge_ref, f32[26,128,128]{2,1,0:T(8,128)S(1)} %get-tuple-element.8.acc_ref, bf16[4096,512]{1,0:T(8,128)(2,1)S(1)} %get-tuple-element.9.split_ref, f32[1648,128]{1,0:T(8,128)S(1)} %collective-permute-done.down_ref, ...), custom_call_target="tpu_custom_call" | custom-call | flops 3000000000 | bytes 9437184 | tf_op jit(solution)/shard_map/halo_products/pallas_call | solution.py:472
  41.7 0.1 collective-permute-start.2
  41.8 2.4 %collective-permute-done.2 = f32[16,104,128]{2,1,0:T(8,128)S(1)} collective-permute-done((f32[16,104,128]{2,1,0:T(8,128)S(1)}, f32[16,104,128]{2,1,0:T(8,128)S(1)}, u32[]{:S(2)}, u32[]{:S(2)}) %collective-permute-start.2) | collective-permute-done | bytes 852000 | tf_op jit(solution)/shard_map/ppermute | solution.py:414
  44.2 0.1 add.12
  44.3 19.0 %all_to_all.15.in_ref = f32[16,104,128]{2,1,0:T(8,128)S(1)} all-to-all(f32[16,104,128]{2,1,0:T(8,128)S(1)} %add.12), channel_id=1, replica_groups={{0,1,2,3,64,65,66,67,128,129,130,131,192,193,194,195},{4,5,6,7,68,69,70..., dimensions={0} | all-to-all | bytes 1703936 | tf_op jit(solution)/shard_map/all_to_all | solution.py:398
  63.3 0.1 add_and_repeat.2
  63.4 16.1 %all_to_all.16.in_ref = f32[8,104,128]{2,1,0:T(8,128)S(1)} all-to-all(f32[8,104,128]{2,1,0:T(8,128)S(1)} %add_and_repeat.2), channel_id=1, replica_groups={{0,4,8,12,16,20,24,28},{1,5,9,13,17,21,25,29},{2,6,10,14,18,22,26,30},{..., dimensions={0} | all-to-all | bytes 851968 | tf_op jit(solution)/shard_map/all_to_all | solution.py:398
  79.5 0.1 add_and_repeat.3
  79.6 15.6 %all_to_all.17.mine_ref = f32[16,104,128]{2,1,0:T(8,128)S(1)} all-to-all(f32[16,104,128]{2,1,0:T(8,128)S(1)} %add_and_repeat.3), channel_id=1, replica_groups={{0,1,2,3,64,65,66,67,128,129,130,131,192,193,194,195},{4,5,6,7,68,69,70..., dimensions={0} | all-to-all | bytes 1703936 | tf_op jit(solution)/shard_map/all_to_all | solution.py:398
  95.2 3.7 %collective-permute-start.3 = (f32[16,104,128]{2,1,0:T(8,128)S(1)}, f32[16,104,128]{2,1,0:T(8,128)S(1)}, u32[]{:S(2)}, u32[]{:S(2)}) collective-permute-start(f32[16,104,128]{2,1,0:T(8,128)S(1)} %all_to_all.17.mine_ref), channel_id=1, source_target_pairs={{0,32},{32,0},{64,96},{96,64},{128,160},{160,128},{192,224},{224,1... | collective-permute-start | bytes 2555912 | tf_op jit(solution)/shard_map/ppermute | solution.py:414
  98.9 2.0 %collective-permute-done.3.other_ref = f32[16,104,128]{2,1,0:T(8,128)S(1)} collective-permute-done((f32[16,104,128]{2,1,0:T(8,128)S(1)}, f32[16,104,128]{2,1,0:T(8,128)S(1)}, u32[]{:S(2)}, u32[]{:S(2)}) %collective-permute-start.3) | collective-permute-done | bytes 852000 | tf_op jit(solution)/shard_map/ppermute | solution.py:414
  100.9 17.5 %factor_and_solve.1 = (f32[512,512]{1,0:T(8,128)}, f32[512,512]{1,0:T(8,128)}) custom-call(s32[3]{0:T(128)S(1)} %pad_add_fusion.edge_ref, f32[16,104,128]{2,1,0:T(8,128)S(1)} %all_to_all.17.mine_ref, f32[16,104,128]{2,1,0:T(8,128)S(1)} %collective-permute-done.3.other_ref), custom_call_target="tpu_custom_call" | custom-call | tf_op jit(solution)/shard_map/factor_and_solve/pallas_call | solution.py:495
Async XLA Ops:
  2.9 35.2 %collective-permute-start = (f32[1648,128]{1,0:T(8,128)}, f32[1648,128]{1,0:T(8,128)S(1)}, u32[]{:S(2)}, u32[]{:S(2)}) collective-permute-start(f32[1648,128]{1,0:T(8,128)} %get-tuple-element.10), channel_id=1, source_target_pairs={{1,0},{2,1},{3,2},{4,3},{5,4},{6,5},{7,6},{8,7},{9,8},{10,9},{11,1... | collective-permute-start | bytes 2531336 | tf_op jit(solution)/shard_map/ppermute | solution.py:392
  13.9 24.2 %collective-permute-start.1 = (f32[1440,128]{1,0:T(8,128)}, f32[1440,128]{1,0:T(8,128)S(1)}, u32[]{:S(2)}, u32[]{:S(2)}) collective-permute-start(f32[1440,128]{1,0:T(8,128)} %get-tuple-element.11), channel_id=1, source_target_pairs={{0,1},{1,2},{2,3},{3,4},{4,5},{5,6},{6,7},{7,8},{8,9},{9,10},{10,1... | collective-permute-start | bytes 2211848 | tf_op jit(solution)/shard_map/ppermute | solution.py:392
  15.9 1.6 %copy-start = (f32[4096,128]{1,0:T(8,128)S(1)}, f32[4096,128]{1,0:T(8,128)}, u32[]{:S(2)}) copy-start(f32[4096,128]{1,0:T(8,128)} %rec_ref.3) | copy-start | bytes 6291460
  41.7 2.5 %collective-permute-start.2 = (f32[16,104,128]{2,1,0:T(8,128)S(1)}, f32[16,104,128]{2,1,0:T(8,128)S(1)}, u32[]{:S(2)}, u32[]{:S(2)}) collective-permute-start(f32[16,104,128]{2,1,0:T(8,128)S(1)} %get-tuple-element.13), channel_id=1, source_target_pairs={{0,32},{32,0},{64,96},{96,64},{128,160},{160,128},{192,224},{224,1... | collective-permute-start | bytes 2555912 | tf_op jit(solution)/shard_map/ppermute | solution.py:414
  95.2 5.7 %collective-permute-start.3 = (f32[16,104,128]{2,1,0:T(8,128)S(1)}, f32[16,104,128]{2,1,0:T(8,128)S(1)}, u32[]{:S(2)}, u32[]{:S(2)}) collective-permute-start(f32[16,104,128]{2,1,0:T(8,128)S(1)} %all_to_all.17.mine_ref), channel_id=1, source_target_pairs={{0,32},{32,0},{64,96},{96,64},{128,160},{160,128},{192,224},{224,1... | collective-permute-start | bytes 2555912 | tf_op jit(solution)/shard_map/ppermute | solution.py:414
